TPU v7x, 256 devices: a whole 4x4x8 slice. The times are simulated.
256 devices in a mesh: section: 4 (over x), mp: 8 (over y, core), dp: 8 (over z).
Axes of the slice: x: 4, y: 4, z: 8, core: 2. Of those that a mesh axis runs over, the one named last changes fastest.
Arguments:
- target_hidden: bfloat16 [8, 256, 8192], P('dp', None, 'section'), may hold values from -43 to 43, as said below
- embeds: bfloat16 [8, 256, 8192], P('dp', None, 'section'), may hold values from -50 to 50, as said below
- token_ids: int32 [8, 256], replicated, may hold values from 0 to 65535
- lengths: int32 [8], replicated, may hold values from 1 to 128, as said below
- offsets: int32 [8], replicated, may hold values from 0 to 128, as said below
- target_gain: float32 [8192], P('section'), may hold values from 0.5 to 1.5
- draft_gain: float32 [8192], P('section'), may hold values from 0.5 to 1.5
- head: bfloat16 [65536, 8192], P(('mp', 'dp'), 'section'), may hold values from -0.1875 to 0.1875
- fc_embed: bfloat16 [8192, 8192], P('section', ('mp', 'dp')), may hold values from -0.046875 to 0.046875
- fc_feature: bfloat16 [8192, 8192], P('section', ('mp', 'dp')), may hold values from -0.046875 to 0.046875
Outputs:
- loss: float32 [], replicated
- grad_embed: float32 [8192, 8192], P('section', ('mp', 'dp'))
- grad_feature: float32 [8192, 8192], P('section', ('mp', 'dp'))
Inputs may be any that keep to these rules, and one draw needn't show every extreme that they name: `lengths`: they sum to 512, and the longest response has exactly 128 rows. offsets + lengths <= 256 in every sequence; the sequence of the longest response starts at 128. `target_hidden`: real-valued features. `embeds`: real-valued embeddings.
All inputs are finite; a program needn't handle non-finite values.
Results may differ from a plain program's by a relative error of at most 0.0035.
The roundings to bfloat16 on the way count: a program that leaves them out, or rounds other values in their place, can miss the bound.
Values may be sent and summed in bfloat16 or wider, within the bound.
A program may use at most 64 MiB of HBM per device.

v0:
```python
import jax
import jax.numpy as jnp
from jax import lax
from jax.sharding import PartitionSpec as P

D = 8192
R_OWN = 8


z_weight = 0.004
label_mix = 0.1
eps_norm = 1e-05


def contract_last(operand, weights):
    return lax.dot_general(
        operand, weights, (((1,), (1,)), ((), ())), preferred_element_type=jnp.float32
    )


def contract_first(operand, weights):
    return lax.dot_general(
        operand, weights, (((0,), (0,)), ((), ())), preferred_element_type=jnp.float32
    )


def sequence_of(packed, starts):
    return jnp.sum((starts[None, :] <= packed[:, None]).astype(jnp.int32), axis=1) - 1


def tile_sums(target_logit, draft_logit, labels, column_zero):
    is_label = (
        labels[:, None] - column_zero == jnp.arange(target_logit.shape[1], dtype=jnp.int32)[None, :]
    )
    target_exp = jnp.exp(target_logit)
    return (
        jnp.sum(target_exp, axis=1),
        jnp.sum(target_exp * draft_logit, axis=1),
        jnp.sum(jnp.exp(draft_logit), axis=1),
        jnp.sum(jnp.where(is_label, draft_logit, 0.0), axis=1),
    )


def tile_grad(target_logit, draft_logit, labels, column_zero, totals):
    target_total, cross_total, draft_total, label_logit = totals
    draft_lse = jnp.log(draft_total)
    target_lse = jnp.log(target_total)
    is_label = (
        labels[:, None] - column_zero == jnp.arange(target_logit.shape[1], dtype=jnp.int32)[None, :]
    )
    logit_grad = (
        (1.0 + 2.0 * z_weight * draft_lse)[:, None] * jnp.exp(draft_logit - draft_lse[:, None])
        - (1.0 - label_mix) * jnp.exp(target_logit - target_lse[:, None])
        - label_mix * is_label.astype(jnp.float32)
    )
    return logit_grad.astype(jnp.bfloat16)


def mean_loss(totals):
    target_total, cross_total, draft_total, label_logit = totals
    draft_lse = jnp.log(draft_total)
    row_loss = (
        draft_lse
        - (1.0 - label_mix) * cross_total / target_total
        - label_mix * label_logit
        + z_weight * draft_lse * draft_lse
    )
    return jnp.mean(row_loss)


def on_device(
    target_hidden,
    embeds,
    token_ids,
    lengths,
    offsets,
    target_gain,
    draft_gain,
    head,
    fc_embed,
    fc_feature,
):
    count_dp = lax.axis_size("dp")
    count_mp = lax.axis_size("mp")
    groups = count_mp * count_dp
    my_dp = lax.axis_index("dp")
    my_mp = lax.axis_index("mp")
    owner_index = my_mp * count_dp + my_dp
    section_index = lax.axis_index("section")
    slice_width = target_hidden.shape[2]
    seq_len = target_hidden.shape[1]
    vocab_tile = head.shape[0]
    slot_count = 2 * R_OWN // count_dp
    total_rows = R_OWN * groups
    starts = jnp.cumsum(lengths) - lengths
    first_row = starts[my_dp]
    my_count = lengths[my_dp]
    my_offset = offsets[my_dp]
    residue = my_mp * count_dp + jnp.arange(count_dp, dtype=jnp.int32)
    first_slot = (first_row - residue + groups - 1) // groups
    packed = (
        groups * (first_slot[:, None] + jnp.arange(slot_count, dtype=jnp.int32)[None, :])
        + residue[:, None]
    )
    is_live = (packed < first_row + my_count).reshape(-1, 1)
    flat_position = jnp.clip(my_offset + packed - first_row, 0, seq_len - 1).reshape(-1)
    taken_embed = jnp.take(embeds[0], flat_position, axis=0)
    taken_feature = jnp.take(target_hidden[0], flat_position, axis=0)
    send_embed = jnp.where(is_live, taken_embed, jnp.zeros_like(taken_embed)).reshape(
        count_dp, slot_count, slice_width
    )
    send_feature = jnp.where(is_live, taken_feature, jnp.zeros_like(taken_feature)).reshape(
        count_dp, slot_count, slice_width
    )
    got_embed, got_feature = (
        lax.all_to_all(send_embed, "dp", split_axis=0, concat_axis=0, tiled=True),
        lax.all_to_all(send_feature, "dp", split_axis=0, concat_axis=0, tiled=True),
    )
    slot_index = jnp.arange(R_OWN, dtype=jnp.int32)
    wanted = groups * slot_index + owner_index
    source = sequence_of(wanted, starts)
    source_first = (starts[source] - owner_index + groups - 1) // groups
    pick_index = source * slot_count + slot_index - source_first
    own_embed = jnp.take(got_embed.reshape(count_dp * slot_count, slice_width), pick_index, axis=0)
    own_feature = jnp.take(
        got_feature.reshape(count_dp * slot_count, slice_width), pick_index, axis=0
    )
    embed_all, feature_all = (
        lax.all_gather(own_embed, ("mp", "dp"), axis=0, tiled=True),
        lax.all_gather(own_feature, ("mp", "dp"), axis=0, tiled=True),
    )
    row_id = jnp.arange(total_rows, dtype=jnp.int32)
    packed_all = groups * (row_id % R_OWN) + row_id // R_OWN
    seq_all = sequence_of(packed_all, starts)
    position_all = offsets[seq_all] + packed_all - starts[seq_all]
    labels = token_ids.reshape(-1)[seq_all * seq_len + position_all]
    target_square = lax.psum(
        jnp.sum(jnp.square(feature_all.astype(jnp.float32)), axis=1), "section"
    )
    target_scale = lax.rsqrt(target_square / D + eps_norm)
    target_norm = (feature_all.astype(jnp.float32) * target_scale[:, None] * target_gain).astype(
        jnp.bfloat16
    )
    partial_value = jnp.dot(embed_all, fc_embed, preferred_element_type=jnp.float32) + jnp.dot(
        feature_all, fc_feature, preferred_element_type=jnp.float32
    )
    summed = lax.psum(partial_value, "section")
    spread = lax.all_to_all(summed, ("mp", "dp"), split_axis=0, concat_axis=1, tiled=True)
    hidden = lax.dynamic_slice_in_dim(spread, section_index * slice_width, slice_width, 1)
    draft_square = lax.psum(jnp.sum(hidden * hidden, axis=1), "section")
    draft_scale = lax.rsqrt(draft_square / D + eps_norm)
    draft_norm = (hidden * draft_scale[:, None] * draft_gain).astype(jnp.bfloat16)
    target_part = contract_last(target_norm, head)
    draft_part = contract_last(lax.all_gather(draft_norm, ("mp", "dp"), axis=0, tiled=True), head)
    target_logit, draft_logit = lax.psum((target_part, draft_part), "section")
    column_zero = owner_index * vocab_tile
    totals = lax.psum(tile_sums(target_logit, draft_logit, labels, column_zero), ("mp", "dp"))
    grad_tile = tile_grad(target_logit, draft_logit, labels, column_zero, totals)
    loss = mean_loss(totals)
    draft_grad = lax.psum_scatter(
        jnp.dot(grad_tile, head, preferred_element_type=jnp.float32),
        ("mp", "dp"),
        scatter_dimension=0,
        tiled=True,
    )
    upstream = draft_grad * draft_gain
    inner_sum = lax.psum(jnp.sum(hidden * upstream, axis=1), "section")
    hidden_grad = (
        draft_scale[:, None] * upstream - hidden * (draft_scale**3 * inner_sum / D)[:, None]
    ).astype(jnp.bfloat16)
    full_grad = lax.all_gather(hidden_grad, "section", axis=1, tiled=True)
    block_grad = lax.all_to_all(full_grad, ("mp", "dp"), split_axis=1, concat_axis=0, tiled=True)
    grad_embed = contract_first(embed_all, block_grad)
    grad_feature = contract_first(feature_all, block_grad)
    return (loss, grad_embed, grad_feature)


def solution(mesh):
    return jax.shard_map(
        on_device,
        mesh=mesh,
        in_specs=(
            P("dp", None, "section"),
            P("dp", None, "section"),
            P(),
            P(),
            P(),
            P("section"),
            P("section"),
            P(("mp", "dp"), "section"),
            P("section", ("mp", "dp")),
            P("section", ("mp", "dp")),
        ),
        out_specs=(P(), P("section", ("mp", "dp")), P("section", ("mp", "dp"))),
        check_vma=False,
    )
```

profile of v0, /device:TPU:1, one launch (start us, length us, event | category | flops | bytes accessed | tf_op | source)
XLA Modules:
  0.0 842.6 jit_solution(10102742475249891229)
XLA Ops:
  7.2 1.4 dynamic_slice.13
  8.6 0.8 reduce-window.9
  9.5 0.7 bitcast_subtract_fusion
  10.1 1.7 fusion.43
  11.8 0.7 and_select_fusion.3
  12.5 1.4 subtract_clamp_fusion
  13.8 0.1 reshape.280
  15.3 0.1 fusion.24
  15.3 0.1 lt.69
  15.5 0.6 gather_fusion.4
  16.1 2.0 gather_fusion.2
  18.1 0.1 select_select_fusion
  18.2 0.7 reshape.273
  18.9 9.0 %all-to-all-start.1 = ((bf16[8,2,2048]{2,1,0:T(2,128)(2,1)}), bf16[8,2,2048]{2,1,0:T(2,128)(2,1)S(1)}, u32[]{:S(2)}, u32[]{:S(2)}) async-start(bf16[8,2,2048]{2,1,0:T(2,128)(2,1)} %reshape.273), calls=%async_computation.1 | async-start | bytes 131072 | tf_op jit(solution)/shard_map/all_to_all | solution.py:117
  27.9 0.2 convert_reduce_fusion.1
  28.1 0.6 gather_fusion
  28.7 0.7 reshape.271
  29.4 5.7 all-to-all-done.1
  35.1 3.4 all-to-all-start
  38.5 0.0 all-gather.4.cloned.1.call-start
  38.6 0.6 gather_fusion.5
  39.2 6.4 all-to-all-done
  45.7 0.6 gather_fusion.3
  46.2 0.7 broadcast_select_fusion
  47.0 0.7 all-gather.6.cloned.1.call-update
  47.8 75.9 %all-gather.4.cloned.1.call-done = bf16[512,2048]{1,0:T(8,128)(2,1)} async-done(((bf16[8,2048]{1,0:T(8,128)(2,1)}), bf16[512,2048]{1,0:T(8,128)(2,1)}) %all-gather.4.cloned.1.call-update) | async-done | bytes 2097168 | tf_op jit(solution)/shard_map/all_gather | solution.py:129
  123.7 2.3 fusion.45
  126.0 76.0 %all-gather.6.cloned.1.call-done = bf16[512,2048]{1,0:T(8,128)(2,1)} async-done(((bf16[8,2048]{1,0:T(8,128)(2,1)}), bf16[512,2048]{1,0:T(8,128)(2,1)}) %all-gather.6.cloned.1.call-update) | async-done | bytes 2097168 | tf_op jit(solution)/shard_map/all_gather | solution.py:130
  202.0 3.2 fusion.7
  205.2 42.0 %all-reduce.8.cloned.1.call-done = f32[64,8,128]{2,1,0:T(8,128)} async-done(((f32[64,8,128]{2,1,0:T(8,128)}), f32[64,8,128]{2,1,0:T(8,128)}) %all-reduce.8.cloned.1.call-update) | async-done | bytes 262160 | tf_op jit(solution)/shard_map/psum | solution.py:147
  247.3 12.8 %all-to-all-start.2 = ((f32[64,8,128]{2,1,0:T(8,128)}), f32[64,8,128]{2,1,0:T(8,128)S(1)}, u32[]{:S(2)}, u32[]{:S(2)}) async-start(f32[64,8,128]{2,1,0:T(8,128)} %all-reduce.8.cloned.1.call-done), calls=%async_computation.2 | async-start | bytes 524288 | tf_op jit(solution)/shard_map/all_to_all | solution.py:148
  260.1 0.0 all-gather.8.cloned.1.call-start
  260.2 0.5 fusion
  260.6 11.5 %all-to-all-done.2 = f32[64,8,128]{2,1,0:T(8,128)S(1)} async-done(((f32[64,8,128]{2,1,0:T(8,128)}), f32[64,8,128]{2,1,0:T(8,128)S(1)}, u32[]{:S(2)}, u32[]{:S(2)}) %all-to-all-start.2) | async-done | bytes 262176 | tf_op jit(solution)/shard_map/all_to_all | solution.py:148
  272.1 0.1 multiply_reduce_fusion.2
  272.2 7.4 all-reduce.2
  279.7 0.7 multiply_convert_fusion
  280.4 0.0 all-reduce.12.cloned.1.call-start
  280.5 5.9 fusion.3
  286.3 68.3 %all-gather.8.cloned.1.call-done = bf16[512,2048]{1,0:T(8,128)(2,1)} async-done(((bf16[8,2048]{1,0:T(8,128)(2,1)}), bf16[512,2048]{1,0:T(8,128)(2,1)}) %all-gather.8.cloned.1.call-update) | async-done | bytes 2097168 | tf_op jit(solution)/shard_map/all_gather | solution.py:154
  354.6 6.5 fusion.46
  361.2 0.0 all-reduce.10.cloned.1.call-start
  361.2 0.6 copy-done.5
  361.9 0.1 convert_reduce_fusion
  362.0 4.3 compare_select_fusion.2
  366.3 4.2 compare_select_fusion.3
  370.6 1.2 broadcast_select_fusion.3
  371.8 3.1 gather_fusion.1
  375.0 81.7 %all-reduce.12.cloned.1.call-done = (f32[512,1024]{1,0:T(8,128)}, f32[512,1024]{1,0:T(8,128)}) async-done(((f32[512,1024]{1,0:T(8,128)}, f32[512,1024]{1,0:T(8,128)}), (f32[512,1024]{1,0:T(8,128)}, f32[512,1024]{1,0:T(8,128)})) %all-reduce.12.cloned.1.call-update) | async-done | bytes 4194320 | tf_op jit(solution)/shard_map/psum | solution.py:155
  456.6 3.2 exponential_reduce_fusion
  459.9 122.9 %all-reduce.1 = (f32[512]{0:T(512)S(1)}, f32[512]{0:T(512)S(1)}, f32[512]{0:T(512)S(1)}, f32[512]{0:T(512)S(1)}) all-reduce(f32[512]{0:T(512)S(1)} %get-tuple-element.6, f32[512]{0:T(512)S(1)} %get-tuple-element.8, f32[512]{0:T(512)S(1)} %get-tuple-element.7, ...), channel_id=1, replica_groups=mesh['section'=4,'mp'=8,'dp'=8] {'mp','dp'}, use_global_device_ids=true, to_apply=%region_17.20 | all-reduce | flops 2048 | bytes 16384 | tf_op jit(solution)/shard_map/psum | solution.py:157
  582.7 0.6 multiply_add_fusion.1
  583.3 8.3 fusion.8
  591.7 0.6 copy-done.7
  592.4 0.6 dynamic-slice
  593.6 192.8 %all-reduce.10.cloned.1.call-done = f32[512,2048]{1,0:T(8,128)} async-done(((f32[512,2048]{1,0:T(8,128)}), f32[512,2048]{1,0:T(8,128)}) %all-reduce.10.cloned.1.call-update) | async-done | bytes 4194320
  786.4 1.0 multiply_reduce_fusion.1
  787.4 8.4 psum.79
  795.8 0.9 subtract_convert_fusion.2
  796.7 9.8 %all_gather.15 = bf16[8,8192]{1,0:T(8,128)(2,1)} all-gather(bf16[8,2048]{1,0:T(8,128)(2,1)S(1)} %subtract_convert_fusion.2), channel_id=1, replica_groups=mesh['section'=4,'mp'=8,'dp'=8] {'section'}, dimensions={1}, use_global_device_ids=true | all-gather | bytes 163840 | tf_op jit(solution)/shard_map/all_gather | solution.py:171
  806.6 14.6 %all-to-all-start.3 = ((bf16[8,64,128]{2,0,1:T(8,128)(2,1)}), bf16[8,64,128]{2,0,1:T(8,128)(2,1)S(1)}, u32[]{:S(2)}, u32[]{:S(2)}) async-start(bf16[8,64,128]{2,0,1:T(8,128)(2,1)} %bitcast.36), calls=%async_computation.3 | async-start | bytes 262144 | tf_op jit(solution)/shard_map/all_to_all | solution.py:172
  821.8 9.3 %all-to-all-done.3 = bf16[8,64,128]{2,0,1:T(8,128)(2,1)S(1)} async-done(((bf16[8,64,128]{2,0,1:T(8,128)(2,1)}), bf16[8,64,128]{2,0,1:T(8,128)(2,1)S(1)}, u32[]{:S(2)}, u32[]{:S(2)}) %all-to-all-start.3) | async-done | bytes 131104 | tf_op jit(solution)/shard_map/all_to_all | solution.py:172
  831.1 1.7 fusion.16
  832.9 1.7 fusion.18
  (42 shorter events, 0.4 us)
Async XLA Ops:
  7.2 8.3 copy-start
  7.2 116.5 %copy-start.3 = (bf16[2048,128]{1,0:T(8,128)(2,1)S(1)}, bf16[2048,128]{1,0:T(8,128)(2,1)}, u32[]{:S(2)}) copy-start(bf16[2048,128]{1,0:T(8,128)(2,1)} %param.22) | copy-start | bytes 1572868
  18.9 16.3 %all-to-all-start.1 = ((bf16[8,2,2048]{2,1,0:T(2,128)(2,1)}), bf16[8,2,2048]{2,1,0:T(2,128)(2,1)S(1)}, u32[]{:S(2)}, u32[]{:S(2)}) async-start(bf16[8,2,2048]{2,1,0:T(2,128)(2,1)} %reshape.273), calls=%async_computation.1 | async-start | bytes 131072 | tf_op jit(solution)/shard_map/all_to_all | solution.py:117
  35.1 10.5 %all-to-all-start = ((bf16[8,2,2048]{2,1,0:T(2,128)(2,1)}), bf16[8,2,2048]{2,1,0:T(2,128)(2,1)S(1)}, u32[]{:S(2)}, u32[]{:S(2)}) async-start(bf16[8,2,2048]{2,1,0:T(2,128)(2,1)} %reshape.271), calls=%async_computation | async-start | bytes 131072 | tf_op jit(solution)/shard_map/all_to_all | solution.py:116
  38.5 85.2 %all-gather.4.cloned.1.call-start = ((), (), s32[]{:S(2)}) async-start(), calls=%async_computation.4 | async-start | bytes 2129920 | tf_op jit(solution)/shard_map/all_gather | solution.py:129
  47.0 155.0 %all-gather.6.cloned.1.call-start = ((), (), s32[]{:S(2)}) async-start(), calls=%async_computation.5 | async-start | bytes 2129920 | tf_op jit(solution)/shard_map/all_gather | solution.py:130
  47.7 199.5 %all-reduce.8.cloned.1.call-start = ((), (), s32[]{:S(2)}) async-start(), calls=%async_computation.6 | async-start | bytes 524288 | tf_op jit(solution)/shard_map/psum | solution.py:147
  202.0 58.2 %copy-start.1 = (bf16[512,2048]{1,0:T(8,128)(2,1)S(1)}, bf16[512,2048]{1,0:T(8,128)(2,1)}, u32[]{:S(2)}) copy-start(bf16[512,2048]{1,0:T(8,128)(2,1)} %all-gather.6.cloned.1.call-done) | copy-start | bytes 6291460
  205.2 74.5 %copy-start.4 = (f32[2048]{0:T(1024)S(1)}, f32[2048]{0:T(1024)}, u32[]{:S(2)}) copy-start(f32[2048]{0:T(1024)} %param.20) | copy-start | bytes 24580
  205.2 75.2 %copy-start.6 = (f32[2048]{0:T(1024)S(1)}, f32[2048]{0:T(1024)}, u32[]{:S(2)}) copy-start(f32[2048]{0:T(1024)} %param.19) | copy-start | bytes 24580
  247.3 24.9 %all-to-all-start.2 = ((f32[64,8,128]{2,1,0:T(8,128)}), f32[64,8,128]{2,1,0:T(8,128)S(1)}, u32[]{:S(2)}, u32[]{:S(2)}) async-start(f32[64,8,128]{2,1,0:T(8,128)} %all-reduce.8.cloned.1.call-done), calls=%async_computation.2 | async-start | bytes 524288 | tf_op jit(solution)/shard_map/all_to_all | solution.py:148
  260.1 94.5 %all-gather.8.cloned.1.call-start = ((), (), s32[]{:S(2)}) async-start(), calls=%async_computation.7 | async-start | bytes 2129920 | tf_op jit(solution)/shard_map/all_gather | solution.py:154
  280.4 176.3 %all-reduce.12.cloned.1.call-start = ((), (), s32[]{:S(2)}) async-start(), calls=%async_computation.9 | async-start | bytes 8388608 | tf_op jit(solution)/shard_map/psum | solution.py:155
  361.2 0.7 copy-start.5
  361.2 425.2 %all-reduce.10.cloned.1.call-start = ((), (), s32[]{:S(2)}) async-start(), calls=%async_computation.8 | async-start | bytes 8388608
  591.7 0.7 copy-start.7
  806.6 24.6 %all-to-all-start.3 = ((bf16[8,64,128]{2,0,1:T(8,128)(2,1)}), bf16[8,64,128]{2,0,1:T(8,128)(2,1)S(1)}, u32[]{:S(2)}, u32[]{:S(2)}) async-start(bf16[8,64,128]{2,0,1:T(8,128)(2,1)} %bitcast.36), calls=%async_computation.3 | async-start | bytes 262144 | tf_op jit(solution)/shard_map/all_to_all | solution.py:172
  831.1 1.7 copy-start.2
Sparse Core Ops, SparseCore 0:
  47.1 76.5 all-gather.3
  127.0 74.8 all-gather.5
  205.3 41.8 all-reduce.7
  280.5 74.0 all-gather.7
  361.3 95.2 all-reduce.11
  591.8 194.5 all-reduce.9
where the time goes:
time: 844 us; the launch traced here: 843 us
  waiting for transfers between devices  570 us (68%)
  blocking collectives  148 us (18%)
  starting transfers between devices  40.1 us (5%)
  matrix products  29.7 us (4%)
  other arithmetic  21.6 us (3%)
  between operations  18.1 us (2%)
  local copies, waits for them, and re-layouts  14.1 us (2%)
    unnamed x7, waiting for transfers between devices  194 us
    psum x1, blocking collectives, on_device(): lax.psum(tile_sums(target_logit, draft_logit, labels, column_zero), ('mp'...  123 us
    psum x1, waiting for transfers between devices, on_device(): target_logit, draft_logit = lax.psum((target_part, draft_part), 'section')  81.7 us
    all_gather x1, waiting for transfers between devices, on_device(): lax.all_gather(own_feature, ('mp', 'dp'), axis=0, tiled=True)  76 us
    all_gather x1, waiting for transfers between devices, on_device(): lax.all_gather(own_embed, ('mp', 'dp'), axis=0, tiled=True)  75.9 us
    all_gather x1, waiting for transfers between devices, on_device(): lax.all_gather(draft_norm, ('mp', 'dp'), axis=0, tiled=True)  68.3 us
    psum x1, waiting for transfers between devices, on_device(): summed = lax.psum(partial_value, 'section')  42 us
  transfers between devices with their start and end apart: 10, of which 10 were waited for; matrix products, arithmetic and copies ran while one was open for 3% of the time, Pallas kernels for 0%

commit v1 on v0

v1 whole, which is shorter than its diff:
```python
import functools

import jax
import jax.numpy as jnp
from jax import lax
from jax.experimental import pallas as pl
from jax.experimental.pallas import tpu as pltpu
from jax.sharding import PartitionSpec as P

MESH = pl.DeviceIdType.MESH
BF = jnp.bfloat16
F32 = jnp.float32
I32 = jnp.int32
CORES = 2
LANES = 128

z_weight = 0.004
label_mix = 0.1
eps_norm = 1e-05


def dot(a, b):
    return jnp.dot(a, b, preferred_element_type=F32)


def dot_last(a, b):
    return lax.dot_general(a, b, (((1,), (1,)), ((), ())), preferred_element_type=F32)


def dot_first(a, b):
    return lax.dot_general(a, b, (((0,), (0,)), ((), ())), preferred_element_type=F32)


def to_rows(columns):
    lane = lax.broadcasted_iota(I32, (LANES, LANES), 1)
    wide = jnp.zeros((LANES, LANES), F32)
    for k, column in enumerate(columns):
        wide = jnp.where(lane == k, column, wide)
    return wide.T[:8]


def to_columns(tile):
    return jnp.concatenate([tile] * (LANES // 8), axis=0).T


class Links:
    def __init__(self, send_sems, recv_sems, peer):
        self.send_sems, self.recv_sems, self.peer = send_sems, recv_sems, peer
        self.tags, self.started = {}, []

    def tag(self, name):
        return self.recv_sems.at[self.tags.setdefault(name, len(self.tags))]

    def send(self, src, dst, device, name, when=None, recv_sem=None):
        copy = pltpu.make_async_remote_copy(
            src_ref=src,
            dst_ref=dst,
            send_sem=self.send_sems.at[len(self.started)],
            recv_sem=self.tag(name) if recv_sem is None else recv_sem,
            device_id=device,
            device_id_type=MESH,
        )
        self.started.append((copy, when))
        if when is None:
            copy.start()
        else:
            pl.when(when)(copy.start)

    def recv(self, dst, name, when=None, recv_sem=None):
        copy = pltpu.make_async_remote_copy(
            src_ref=dst,
            dst_ref=dst,
            send_sem=self.send_sems.at[0],
            recv_sem=self.tag(name) if recv_sem is None else recv_sem,
            device_id=self.peer,
            device_id_type=MESH,
        )
        if when is None:
            copy.wait_recv()
        else:
            pl.when(when)(copy.wait_recv)

    def finish(self):
        for copy, when in self.started:
            if when is None:
                copy.wait_send()
            else:
                pl.when(when)(copy.wait_send)


def kernel(
    sizes,
    lengths_ref, offsets_ref, tokens_ref, tgain_ref, dgain_ref,
    feat_hbm, emb_hbm, head_hbm, fce_hbm, fcf_hbm,
    loss_ref, ge_ref, gf_ref,
    ebuf, fbuf, head, fce, fcf, pk, rk, rows_all,
    hpart, hrecv, hmine, hblk, tq, tnorm, dnorm,
    tl, tl_a, tl_b, dl, dl_a, dl_b, arbuf, lossbuf,
    lgrad, dg, dg_in, dg_a, dg_b, dz, dz_a, dz_b, hg_out, hg,
    send_sems, recv_sems, local_sems,
):
    X, M, Z, R = sizes
    C = CORES
    Y = M // C
    seqs, seq_len = tokens_ref.shape
    width = head.shape[1]
    vocab = head.shape[0]
    KC = width // M
    SL = rk.shape[0] // Z
    GROUP = R // Z
    Q = R // X
    depth = width * X
    x, m, z = lax.axis_index("section"), lax.axis_index("mp"), lax.axis_index("dp")
    y, c = m // C, m % C
    d = 1 - 2 * c
    ln = Links(send_sems, recv_sems, (x, m + 1 - 2 * c, z))

    def around(me, o, n):
        return lax.rem(me + o + 2 * n, n)

    def turn(me, o, n):
        return lax.rem(me + o * d + 2 * n, n)

    mine = pl.ds(pl.multiple_of(m * KC, KC), KC)
    loads = [
        pltpu.make_async_copy(emb_hbm.at[0, :, mine], ebuf, local_sems.at[0]),
        pltpu.make_async_copy(feat_hbm.at[0, :, mine], fbuf, local_sems.at[1]),
        pltpu.make_async_copy(fce_hbm, fce, local_sems.at[2]),
        pltpu.make_async_copy(fcf_hbm, fcf, local_sems.at[3]),
        pltpu.make_async_copy(head_hbm, head, local_sems.at[4]),
    ]
    for load in loads:
        load.start()

    barrier = pltpu.get_barrier_semaphore()

    def greet(device):
        pl.semaphore_signal(barrier, inc=1, device_id=device, device_id_type=MESH)

    for o in range(1, Z):
        greet((x, m, around(z, o, Z)))
    for o in range(1, M):
        greet((x, around(m, o, M), z))
    own_xc = x * C + c
    for o in range(1, X * C):
        g = around(own_xc, o, X * C)
        greet((g // C, y * C + g % C, z))
    off_diagonal = x != y
    pl.when(off_diagonal)(lambda: greet((y, x * C + c, z)))
    for o in range(Y):
        q = around(y, o, Y)
        if o == 0:
            pl.when(off_diagonal)(lambda q=q: greet((y, q * C + c, z)))
        else:
            greet((y, q * C + c, z))
    steady = (Z - 1) + (M - 1) + (X * C - 1) + (X - 1)
    pl.semaphore_wait(barrier, steady + 2 * off_diagonal.astype(I32))

    start, total = [], jnp.int32(0)
    for k in range(seqs):
        start.append(total)
        total = total + lengths_ref[k]
    my_start, my_count, my_offset = jnp.int32(0), lengths_ref[z], offsets_ref[z]
    for k in range(seqs):
        my_start = my_start + jnp.where(k < z, lengths_ref[k], 0)

    slot = lax.broadcasted_iota(I32, (Z * SL, seq_len), 0)
    place = lax.broadcasted_iota(I32, (Z * SL, seq_len), 1)
    group = slot // SL
    packed = my_start + ((group - my_start) & (Z - 1)) + Z * (slot - group * SL)
    live = packed < my_start + my_count
    pick = jnp.where(live & (place == my_offset + packed - my_start), 1.0, 0.0).astype(BF)
    loads[0].wait()
    pk[:, :KC] = dot(pick, ebuf[...]).astype(BF)
    loads[1].wait()
    pk[:, KC:] = dot(pick, fbuf[...]).astype(BF)

    def slots(k):
        return pl.ds(pl.multiple_of(k * SL, SL), SL)

    for o in range(1, Z):
        to = around(z, o, Z)
        ln.send(pk.at[slots(to)], rk.at[slots(z)], (x, m, to), ("deal", o))
    rk[slots(z), :] = pk[slots(z), :]
    want = lax.broadcasted_iota(I32, (GROUP, Z * SL), 0) * Z + z
    slot = lax.broadcasted_iota(I32, (GROUP, Z * SL), 1)
    group = slot // SL
    first = jnp.zeros_like(slot)
    stop = jnp.zeros_like(slot)
    for k in range(seqs):
        first = jnp.where(group == k, start[k], first)
        stop = jnp.where(group == k, start[k] + lengths_ref[k], stop)
    have = first + ((z - first) & (Z - 1)) + Z * (slot - group * SL)
    pick = jnp.where((have == want) & (have < stop), 1.0, 0.0).astype(BF)
    for o in range(1, Z):
        ln.recv(rk.at[slots(around(z, -o, Z))], ("deal", o))
    my_rows = pl.ds(pl.multiple_of(z * GROUP, GROUP), GROUP)
    rows_all[m, my_rows, :] = dot(pick, rk[...]).astype(BF)

    def plane_gather(name, view):
        half = Z // 2
        halfy = Y // 2
        sibling = (x, y * C + 1 - c, z)

        def at_z(o):
            return turn(z, o, Z)

        def at_y(a):
            return turn(y, a, Y)

        def z_pass(k):
            v = view(y, c, at_z(-(k - 1)))
            ln.send(v, v, (x, m, at_z(1)), (name, "z+", k))
            if k < half:
                v = view(y, c, at_z(k - 1))
                ln.send(v, v, (x, m, at_z(-1)), (name, "z-", k))

        def across(a, o):
            v = view(at_y(a), c, at_z(o))
            ln.send(v, v, sibling, (name, "core", -a % Y, -o % Z))

        def spread(o):
            v = view(y, c, at_z(o))
            ln.send(v, v, (x, at_y(1) * C + c, z), (name, "y+", o % Z))
            if halfy > 1:
                ln.send(v, v, (x, at_y(-1) * C + c, z), (name, "y-", o % Z))
            across(0, o)

        def from_y(o):
            v = view(at_y(-1), c, at_z(o))
            ln.recv(v, (name, "y+", o % Z))
            if halfy > 1:
                ln.send(v, v, (x, at_y(1) * C + c, z), (name, "y2", o % Z))
            across(-1, o)
            if halfy > 1:
                v = view(at_y(1), c, at_z(o))
                ln.recv(v, (name, "y-", o % Z))
                across(1, o)

        def from_y2(o):
            if halfy > 1:
                ln.recv(view(at_y(2), c, at_z(o)), (name, "y2", o % Z))
                across(2, o)

        waves = [[0]] + [[-k, k] for k in range(1, half)] + [[-half]]
        z_pass(1)
        spread(0)
        for k in range(1, half + 3):
            if k <= half:
                for o in waves[k]:
                    ln.recv(view(y, c, at_z(o)), (name, "z+" if o < 0 else "z-", abs(o)))
                if k < half:
                    z_pass(k + 1)
                for o in waves[k]:
                    spread(o)
            if 0 <= k - 1 <= half:
                for o in waves[k - 1]:
                    from_y(o)
            if 0 <= k - 2 <= half:
                for o in waves[k - 2]:
                    from_y2(o)
        for wave in waves:
            for o in wave:
                for a in range(Y):
                    ln.recv(view(at_y(a), 1 - c, at_z(o)), (name, "core", a % Y, o % Z))

    def ring_sum(name, me, n, device, chunk, from_up, from_down, produce):
        half = n // 2
        for k in range(1, half + 1):
            i = turn(me, half - k + 1, n)
            produce(i)
            if k > 1:
                ln.recv(from_up.at[k - 2], (name, "up", k - 1))
                chunk(i)[...] += from_up[k - 2]
            ln.send(chunk(i), from_up.at[k - 1], device(turn(me, 1, n)), (name, "up", k))
            if k < half:
                i = turn(me, -(half - k), n)
                produce(i)
                if k > 1:
                    ln.recv(from_down.at[k - 2], (name, "down", k - 1))
                    chunk(i)[...] += from_down[k - 2]
                ln.send(chunk(i), from_down.at[k - 1], device(turn(me, -1, n)), (name, "down", k))
        produce(me)

        def finish():
            ln.recv(from_up.at[half - 1], (name, "up", half))
            summed = chunk(me)[...] + from_up[half - 1]
            if half > 1:
                ln.recv(from_down.at[half - 2], (name, "down", half - 1))
                summed = summed + from_down[half - 2]
            return summed

        return finish

    def add_up(name, tile, base, n2, me2, device2):
        arbuf[base + z] = tile
        for o in range(1, Z):
            ln.send(arbuf.at[base + z], arbuf.at[base + z], (x, m, around(z, o, Z)), (name, 1, o))

        def second():
            for o in range(1, Z):
                ln.recv(arbuf.at[base + around(z, -o, Z)], (name, 1, o))
            part = arbuf[base]
            for k in range(1, Z):
                part = part + arbuf[base + k]
            arbuf[base + Z + me2] = part
            for o in range(1, n2):
                v = arbuf.at[base + Z + me2]
                ln.send(v, v, device2(around(me2, o, n2)), (name, 2, o))

            def finish():
                for o in range(1, n2):
                    ln.recv(arbuf.at[base + Z + around(me2, -o, n2)], (name, 2, o))
                part = arbuf[base + Z]
                for k in range(1, n2):
                    part = part + arbuf[base + Z + k]
                return part

            return finish

        return second

    def xc_device(g):
        return (g // C, y * C + g % C, z)

    plane_gather("rows", lambda yy, cc, zz: rows_all.at[yy * C + cc, pl.ds(pl.multiple_of(zz * GROUP, GROUP), GROUP)])

    loads[2].wait()
    loads[3].wait()

    def rows_of(i):
        return pl.ds(pl.multiple_of(i * Q, Q), Q)

    def project(i, carry):
        acc = jnp.zeros((Q, LANES), F32)
        for k in range(M):
            acc = acc + dot(rows_all[k, rows_of(i), :KC], fce[k * KC:(k + 1) * KC, :])
            acc = acc + dot(rows_all[k, rows_of(i), KC:], fcf[k * KC:(k + 1) * KC, :])
        hpart[i] = acc
        return carry

    lax.fori_loop(0, X, project, 0)
    for o in range(1, X):
        to = around(x, o, X)
        ln.send(hpart.at[to], hrecv.at[x], (to, m, z), ("hidden", o))

    def square(i, carry):
        acc = jnp.zeros((Q, KC), F32)
        for k in range(M):
            f = rows_all[k, rows_of(i), KC:].astype(F32)
            acc = acc + f * f
        tq[x, i] = to_rows([jnp.sum(acc, axis=1, keepdims=True)])
        return carry

    lax.fori_loop(0, X, square, 0)
    for o in range(1, X):
        ln.send(tq.at[x], tq.at[x], (around(x, o, X), m, z), ("square", o))

    hrecv[x] = hpart[x]
    for o in range(1, X):
        ln.recv(hrecv.at[around(x, -o, X)], ("hidden", o))
    hsum = hrecv[0]
    for k in range(1, X):
        hsum = hsum + hrecv[k]
    hmine[...] = hsum
    ln.send(hmine, hblk, (y, x * C + c, z), "swap", when=off_diagonal)

    @pl.when(x == y)
    def _():
        hblk[...] = hmine[...]

    for o in range(1, X):
        ln.recv(tq.at[around(x, -o, X)], ("square", o))

    def normalize(i, carry):
        tile = tq[0, i]
        for k in range(1, X):
            tile = tile + tq[k, i]
        scale = lax.rsqrt(to_columns(tile)[:, :1] / depth + eps_norm)
        for k in range(M):
            f = rows_all[k, rows_of(i), KC:].astype(F32)
            tnorm[rows_of(i), k * KC:(k + 1) * KC] = (f * scale * tgain_ref[:, k * KC:(k + 1) * KC]).astype(BF)
        return carry

    ln.recv(hblk, "swap", when=off_diagonal)
    hid = hblk[...]
    second = add_up("dsq", to_rows([jnp.sum(hid * hid, axis=1, keepdims=True)]), 0, X * C, own_xc, xc_device)
    lax.fori_loop(0, X, normalize, 0)
    finish = second()
    loads[4].wait()

    def target_part(i):
        tl[i] = dot_last(tnorm[rows_of(i), :], head[...])

    def draft_part(i):
        dl[i] = dot_last(dnorm[rows_of(i), :], head[...])

    def x_device(i):
        return (i, m, z)

    draft_square = to_columns(finish())[:, :1]
    dscale = lax.rsqrt(draft_square / depth + eps_norm)
    block = c * Z + z
    dgain = dgain_ref[pl.ds(block, 1), :]

    def norm_view(yy, cc, zz):
        return dnorm.at[rows_of(yy), pl.ds(pl.multiple_of((cc * Z + zz) * LANES, LANES), LANES)]

    norm_view(y, c, z)[...] = (hid * dscale * dgain).astype(BF)
    target_sum = ring_sum("tl", x, X, x_device, lambda i: tl.at[i], tl_a, tl_b, target_part)
    plane_gather("norm", norm_view)

    draft_sum = ring_sum("dl", x, X, x_device, lambda i: dl.at[i], dl_a, dl_b, draft_part)
    target_logit = target_sum()
    draft_logit = draft_sum()

    local = lax.broadcasted_iota(I32, (Q, 1), 0) + x * Q
    packed = Z * (local % GROUP) + local // GROUP
    labels = jnp.zeros((Q, 1), I32)
    lane = lax.broadcasted_iota(I32, (Q, seq_len), 1)
    for k in range(seqs):
        inside = (packed >= start[k]) & (packed < start[k] + lengths_ref[k])
        position = jnp.where(inside, offsets_ref[k] + packed - start[k], -1)
        token = jnp.where(lane == position, tokens_ref[k:k + 1, :], 0)
        labels = labels + jnp.sum(token, axis=1, keepdims=True)
    column = lax.broadcasted_iota(I32, (Q, vocab), 1) + (m * Z + z) * vocab
    is_label = column == labels
    target_exp = jnp.exp(target_logit)
    sums = to_rows([
        jnp.sum(target_exp, axis=1, keepdims=True),
        jnp.sum(target_exp * draft_logit, axis=1, keepdims=True),
        jnp.sum(jnp.exp(draft_logit), axis=1, keepdims=True),
        jnp.sum(jnp.where(is_label, draft_logit, 0.0), axis=1, keepdims=True),
    ])
    base = Z + X * C
    sums = add_up("sums", sums, base, M, m, lambda g: (x, g, z))()()
    columns = to_columns(sums)
    target_lse = jnp.log(columns[:, 0:1])
    draft_lse = jnp.log(columns[:, 2:3])
    grad = (
        (1.0 + 2.0 * z_weight * draft_lse) * jnp.exp(draft_logit - draft_lse)
        - (1.0 - label_mix) * jnp.exp(target_logit - target_lse)
        - label_mix * is_label.astype(F32)
    )
    lgrad[x] = grad.astype(BF)

    v = lgrad.at[x]
    ln.send(v, v, x_device(turn(x, 1, X)), ("lg", 1))
    if X > 2:
        ln.send(v, v, x_device(turn(x, -1, X)), ("lg", -1))

    lse_row = jnp.log(sums[2:3])
    row_loss = (
        lse_row
        - (1.0 - label_mix) * sums[1:2] / sums[0:1]
        - label_mix * sums[3:4]
        + z_weight * lse_row * lse_row
    )
    lossbuf[x] = jnp.broadcast_to(row_loss, (8, LANES))
    for o in range(1, X):
        ln.send(lossbuf.at[x], lossbuf.at[x], (around(x, o, X), m, z), ("loss", o))

    v = lgrad.at[turn(x, -1, X)]
    ln.recv(v, ("lg", 1))
    if X > 2:
        ln.send(v, v, x_device(turn(x, 1, X)), ("lg", 2))
        ln.recv(lgrad.at[turn(x, 1, X)], ("lg", -1))
        ln.recv(lgrad.at[turn(x, 2, X)], ("lg", 2))

    side = Z * LANES

    def grad_part(half, i):
        dg[half, i] = dot(lgrad[i], head[:, pl.ds(pl.multiple_of(half * side, side), side)])

    sibling = (x, y * C + 1 - c, z)
    for o in ([2, 1, -1, 0] if Y > 2 else [1, 0]):
        i = turn(y, o, Y)
        grad_part(1 - c, i)
        ln.send(dg.at[1 - c, i], dg_in.at[i], sibling, ("dgc", -o % Y))

    def own_part(i, o):
        grad_part(c, i)
        ln.recv(dg_in.at[i], ("dgc", o % Y))
        dg[c, i] += dg_in[i]

    todo = iter([2, -1, 1, 0] if Y > 2 else [1, 0])
    summed = ring_sum(
        "dgy", y, Y, lambda i: (x, i * C + c, z), lambda i: dg.at[c, i], dg_a, dg_b, lambda i: own_part(i, next(todo))
    )()
    for k in range(Z):
        dz[k] = summed[:, k * LANES:(k + 1) * LANES]
    dgrad = ring_sum("dgz", z, Z, lambda i: (x, m, i), lambda i: dz.at[i], dz_a, dz_b, lambda i: None)()

    upstream = dgrad * dgain
    hid = hblk[...]
    base = base + Z + M
    inner = add_up("inner", to_rows([jnp.sum(hid * upstream, axis=1, keepdims=True)]), base, X * C, own_xc, xc_device)()()
    inner = to_columns(inner)[:, :1]
    hgrad = (dscale * upstream - hid * (dscale * dscale * dscale * inner / depth)).astype(BF)
    hg_out[...] = hgrad
    names = [("hg", q) for q in range(Y)]
    first_name = len(ln.tags)
    for name in names:
        ln.tag(name)
    for o in range(X):
        ln.send(
            hg_out, hg.at[y], (around(x, o, X), x * C + c, z), None,
            when=off_diagonal if o == 0 else None, recv_sem=recv_sems.at[first_name + y],
        )

    @pl.when(x == y)
    def _():
        hg[y] = hgrad

    for o in range(1, X):
        ln.recv(lossbuf.at[around(x, -o, X)], ("loss", o))
    part = lossbuf[0]
    for k in range(1, X):
        part = part + lossbuf[k]
    loss_ref[0, 0] = jnp.sum(part[:1]) / R

    for o in range(Y):
        q = around(y, o, Y)
        ln.recv(hg.at[q], None, when=off_diagonal if o == 0 else None, recv_sem=recv_sems.at[first_name + q])
    block_grad = hg[...].reshape(R, LANES)

    def outer(k, carry):
        at = pl.ds(pl.multiple_of(k * KC, KC), KC)
        ge_ref[at, :] = dot_first(rows_all[k, :, :KC], block_grad)
        gf_ref[at, :] = dot_first(rows_all[k, :, KC:], block_grad)
        return carry

    lax.fori_loop(0, M, outer, 0)
    ln.finish()


def on_device(
    target_hidden,
    embeds,
    token_ids,
    lengths,
    offsets,
    target_gain,
    draft_gain,
    head,
    fc_embed,
    fc_feature,
    total_rows,
    most_rows,
):
    X, M, Z = lax.axis_size("section"), lax.axis_size("mp"), lax.axis_size("dp")
    C = CORES
    Y = M // C
    R = total_rows
    Q = R // X
    vocab, width = head.shape
    seq_len = embeds.shape[1]
    KC = width // M
    SL = most_rows // Z
    half = X // 2
    rest = max(1, half - 1)
    halfy = Y // 2
    halfz = Z // 2
    side = Z * LANES
    V = pltpu.VMEM
    scratch = [
        V((seq_len, KC), BF), V((seq_len, KC), BF), V((vocab, width), BF), V((width, LANES), BF), V((width, LANES), BF),
        V((Z * SL, 2 * KC), BF), V((Z * SL, 2 * KC), BF), V((M, R, 2 * KC), BF),
        V((X, Q, LANES), F32), V((X, Q, LANES), F32), V((Q, LANES), F32), V((Q, LANES), F32),
        V((X, X, 8, LANES), F32), V((R, width), BF), V((R, width), BF),
        V((X, Q, vocab), F32), V((half, Q, vocab), F32), V((rest, Q, vocab), F32),
        V((X, Q, vocab), F32), V((half, Q, vocab), F32), V((rest, Q, vocab), F32),
        V((3 * Z + 2 * X * C + M, 8, LANES), F32), V((X, 8, LANES), F32),
        V((X, Q, vocab), BF),
        V((C, Y, Q, side), F32), V((Y, Q, side), F32),
        V((halfy, Q, side), F32), V((max(1, halfy - 1), Q, side), F32),
        V((Z, Q, LANES), F32), V((halfz, Q, LANES), F32), V((max(1, halfz - 1), Q, LANES), F32),
        V((Q, LANES), BF), V((Y, Q, LANES), BF),
        pltpu.SemaphoreType.DMA((224,)), pltpu.SemaphoreType.DMA((224,)), pltpu.SemaphoreType.DMA((5,)),
    ]
    smem = pl.BlockSpec(memory_space=pltpu.SMEM)
    vmem = pl.BlockSpec(memory_space=pltpu.VMEM)
    hbm = pl.BlockSpec(memory_space=pl.ANY)
    loss, grad_embed, grad_feature = pl.pallas_call(
        functools.partial(kernel, (X, M, Z, R)),
        out_shape=(
            jax.ShapeDtypeStruct((1, 1), F32),
            jax.ShapeDtypeStruct((width, LANES), F32),
            jax.ShapeDtypeStruct((width, LANES), F32),
        ),
        in_specs=[smem, smem, vmem, vmem, vmem, hbm, hbm, hbm, hbm, hbm],
        out_specs=(smem, vmem, vmem),
        scratch_shapes=scratch,
        compiler_params=pltpu.CompilerParams(
            collective_id=0, has_side_effects=True, vmem_limit_bytes=56 * 1024 * 1024
        ),
        cost_estimate=pl.CostEstimate(flops=7_500_000_000, bytes_accessed=10_000_000, transcendentals=1_000_000),
    )(
        lengths, offsets, token_ids, target_gain.reshape(1, width), draft_gain.reshape(width // LANES, LANES),
        target_hidden, embeds, head, fc_embed, fc_feature,
    )
    return loss[0, 0], grad_embed, grad_feature


def solution(mesh, total_rows=512, most_rows=128):
    return jax.shard_map(
        functools.partial(on_device, total_rows=total_rows, most_rows=most_rows),
        mesh=mesh,
        in_specs=(
            P("dp", None, "section"),
            P("dp", None, "section"),
            P(),
            P(),
            P(),
            P("section"),
            P("section"),
            P(("mp", "dp"), "section"),
            P("section", ("mp", "dp")),
            P("section", ("mp", "dp")),
        ),
        out_specs=(P(), P("section", ("mp", "dp")), P("section", ("mp", "dp"))),
        check_vma=False,
    )
```

time: 844 us -> 211 us (0.25)
  waiting for transfers between devices: 570 us -> 0 us
  Pallas kernels: 0 us -> 202 us
  blocking collectives: 148 us -> 0 us
  starting transfers between devices: 40.1 us -> 0 us
  matrix products: 29.7 us -> 0 us
  other arithmetic: 21.6 us -> 0 us
  between operations: 18.1 us -> 2.38 us
  local copies, waits for them, and re-layouts: 14.1 us -> 4.52 us
    all_gather x3 -> x0, waiting for transfers between devices: 220 us -> none  [the longest x1 76 us: on_device(): lax.all_gather(own_feature, ('mp', 'dp'), axis=0, tiled=True)]
    pallas_call x0 -> x1, Pallas kernels: none -> 202 us  [on_device(): pl.pallas_call(functools.partial(kernel, (X, M, Z, R)), out_shape=(jax.Sh...]
    unnamed x7 -> x0, waiting for transfers between devices: 194 us -> none
    psum x3 -> x0, blocking collectives: 139 us -> none  [the longest x1 123 us: on_device(): lax.psum(tile_sums(target_logit, draft_logit, labels, column_zero), ('mp'...]
    psum x2 -> x0, waiting for transfers between devices: 124 us -> none  [the longest x1 81.7 us: on_device(): target_logit, draft_logit = lax.psum((target_part, draft_part), 'section')]
    all_to_all x4 -> x0, starting transfers between devices: 39.8 us -> none  [the longest x1 14.6 us: on_device(): lax.all_to_all(full_grad, ('mp', 'dp'), split_axis=1, concat_axis=0, tile...]
    all_to_all x4 -> x0, waiting for transfers between devices: 32.9 us -> none  [the longest x1 11.5 us: on_device(): lax.all_to_all(summed, ('mp', 'dp'), split_axis=0, concat_axis=1, tiled=T...]
    dot_general x7 -> x0, matrix products: 29.7 us -> none  [the longest x2 12.4 us: contract_last(): lax.dot_general(operand, weights, (((1,), (1,)), ((), ())), preferred_ele...]
  transfers between devices with their start and end apart: 10 -> 0, of which waited for: 10 -> 0; matrix products, arithmetic and copies ran while one was open for 3% -> 0% of each run, Pallas kernels for 0% -> 0%
where the time goes in v1:
time: 211 us; the launch traced here: 209 us
  Pallas kernels  202 us (96%)
  local copies, waits for them, and re-layouts  4.52 us (2%)
  between operations  2.38 us (1%)
    pallas_call x1, Pallas kernels, on_device(): pl.pallas_call(functools.partial(kernel, (X, M, Z, R)), out_shape=(jax.Sh...  202 us
    unnamed x2, local copies, waits for them, and re-layouts  4.52 us

profile of v1, /device:TPU:1, one launch (start us, length us, event | category | flops | bytes accessed | tf_op | source)
XLA Modules:
  0.0 208.7 jit_solution(12280597654884959420)
XLA Ops:
  0.6 201.8 %shard_map.121 = (f32[1,1]{1,0:T(1,128)}, f32[2048,128]{1,0:T(8,128)}, f32[2048,128]{1,0:T(8,128)}) custom-call(s32[8]{0:T(128)} %lengths_ref.1, s32[8]{0:T(128)} %offsets_ref.1, s32[8,256]{1,0:T(8,128)} %tokens_ref.1, f32[1,2048]{1,0:T(1,128)} %bitcast.3, f32[16,128]{1,0:T(8,128)} %bitcast.4, bf16[1,256,2048]{2,1,0:T(8,128)(2,1)} %feat_hbm.1, ...), custom_call_target="tpu_custom_call" | custom-call | flops 7500000256 | bytes 10000000 | tf_op jit(solution)/shard_map/pallas_call | solution.py:584
  203.1 2.3 %copy.17 = f32[2048,128]{1,0:T(8,128)} copy(f32[2048,128]{1,0:T(8,128)} %get-tuple-element.13) | data formatting | bytes 2097152
  205.3 2.3 %copy.18 = f32[2048,128]{1,0:T(8,128)} copy(f32[2048,128]{1,0:T(8,128)} %get-tuple-element.14) | data formatting | bytes 2097152

commit v2 on v1

--- a/solution.py
+++ b/solution.py
@@ -93,27 +93,30 @@
     lengths_ref, offsets_ref, tokens_ref, tgain_ref, dgain_ref,
     feat_hbm, emb_hbm, head_hbm, fce_hbm, fcf_hbm,
     loss_ref, ge_ref, gf_ref,
-    ebuf, fbuf, head, fce, fcf, pk, rk, rows_all,
+    ebuf, fbuf, head, fce, fcf, pk, rk, ef,
     hpart, hrecv, hmine, hblk, tq, tnorm, dnorm,
-    tl, tl_a, tl_b, dl, dl_a, dl_b, arbuf, lossbuf,
-    lgrad, dg, dg_in, dg_a, dg_b, dz, dz_a, dz_b, hg_out, hg,
+    tl, tl_up, tl_down, dl, dl_up, dl_down, arbuf, lossbuf,
+    lgrad, dg, dg_in, dg_up, dg_down, dz, dz_up, dz_down, hg_out, hg,
     send_sems, recv_sems, local_sems,
 ):
     X, M, Z, R = sizes
     C = CORES
     Y = M // C
     seqs, seq_len = tokens_ref.shape
-    width = head.shape[1]
-    vocab = head.shape[0]
+    vocab, width = head.shape
     KC = width // M
     SL = rk.shape[0] // Z
     GROUP = R // Z
     Q = R // X
+    H = Q // 2
+    HALF = R // 2
     depth = width * X
+    side = Z * LANES
     x, m, z = lax.axis_index("section"), lax.axis_index("mp"), lax.axis_index("dp")
     y, c = m // C, m % C
     d = 1 - 2 * c
-    ln = Links(send_sems, recv_sems, (x, m + 1 - 2 * c, z))
+    sibling = (x, y * C + 1 - c, z)
+    ln = Links(send_sems, recv_sems, sibling)
 
     def around(me, o, n):
         return lax.rem(me + o + 2 * n, n)
@@ -195,12 +198,13 @@
     for o in range(1, Z):
         ln.recv(rk.at[slots(around(z, -o, Z))], ("deal", o))
     my_rows = pl.ds(pl.multiple_of(z * GROUP, GROUP), GROUP)
-    rows_all[m, my_rows, :] = dot(pick, rk[...]).astype(BF)
-
-    def plane_gather(name, view):
+    dealt = dot(pick, rk[...]).astype(BF)
+    ef[0, my_rows, mine] = dealt[:, :KC]
+    ef[1, my_rows, mine] = dealt[:, KC:]
+
+    def plane_gather(name, view, beside=None):
         half = Z // 2
         halfy = Y // 2
-        sibling = (x, y * C + 1 - c, z)
 
         def at_z(o):
             return turn(z, o, Z)
@@ -259,38 +263,46 @@
             if 0 <= k - 2 <= half:
                 for o in waves[k - 2]:
                     from_y2(o)
+            if beside and k in beside:
+                beside[k]()
         for wave in waves:
             for o in wave:
                 for a in range(Y):
                     ln.recv(view(at_y(a), 1 - c, at_z(o)), (name, "core", a % Y, o % Z))
 
-    def ring_sum(name, me, n, device, chunk, from_up, from_down, produce):
-        half = n // 2
-        for k in range(1, half + 1):
-            i = turn(me, half - k + 1, n)
-            produce(i)
+    class Ring:
+        def __init__(self, name, me, n, device, chunk, up, down):
+            self.name, self.me, self.n, self.device = name, me, n, device
+            self.chunk, self.from_up, self.from_down = chunk, up, down
+
+        def up(self, k):
+            half = self.n // 2
+            if k > half:
+                return
+            mine = self.chunk(turn(self.me, half - k + 1, self.n))
             if k > 1:
-                ln.recv(from_up.at[k - 2], (name, "up", k - 1))
-                chunk(i)[...] += from_up[k - 2]
-            ln.send(chunk(i), from_up.at[k - 1], device(turn(me, 1, n)), (name, "up", k))
-            if k < half:
-                i = turn(me, -(half - k), n)
-                produce(i)
-                if k > 1:
-                    ln.recv(from_down.at[k - 2], (name, "down", k - 1))
-                    chunk(i)[...] += from_down[k - 2]
-                ln.send(chunk(i), from_down.at[k - 1], device(turn(me, -1, n)), (name, "down", k))
-        produce(me)
-
-        def finish():
-            ln.recv(from_up.at[half - 1], (name, "up", half))
-            summed = chunk(me)[...] + from_up[half - 1]
+                ln.recv(self.from_up(k - 2), (self.name, "up", k - 1))
+                mine[...] += self.from_up(k - 2)[...]
+            ln.send(mine, self.from_up(k - 1), self.device(turn(self.me, 1, self.n)), (self.name, "up", k))
+
+        def down(self, k):
+            half = self.n // 2
+            if k >= half:
+                return
+            mine = self.chunk(turn(self.me, k - half, self.n))
+            if k > 1:
+                ln.recv(self.from_down(k - 2), (self.name, "down", k - 1))
+                mine[...] += self.from_down(k - 2)[...]
+            ln.send(mine, self.from_down(k - 1), self.device(turn(self.me, -1, self.n)), (self.name, "down", k))
+
+        def finish(self):
+            half = self.n // 2
+            total = self.chunk(self.me)[...]
             if half > 1:
-                ln.recv(from_down.at[half - 2], (name, "down", half - 1))
-                summed = summed + from_down[half - 2]
-            return summed
-
-        return finish
+                ln.recv(self.from_down(half - 2), (self.name, "down", half - 1))
+                total = total + self.from_down(half - 2)[...]
+            ln.recv(self.from_up(half - 1), (self.name, "up", half))
+            return total + self.from_up(half - 1)[...]
 
     def add_up(name, tile, base, n2, me2, device2):
         arbuf[base + z] = tile
@@ -323,54 +335,46 @@
     def xc_device(g):
         return (g // C, y * C + g % C, z)
 
-    plane_gather("rows", lambda yy, cc, zz: rows_all.at[yy * C + cc, pl.ds(pl.multiple_of(zz * GROUP, GROUP), GROUP)])
+    def rows_view(yy, cc, zz):
+        rows = pl.ds(pl.multiple_of(zz * GROUP, GROUP), GROUP)
+        return ef.at[:, rows, pl.ds(pl.multiple_of((yy * C + cc) * KC, KC), KC)]
+
+    plane_gather("rows", rows_view)
 
     loads[2].wait()
     loads[3].wait()
-
-    def rows_of(i):
-        return pl.ds(pl.multiple_of(i * Q, Q), Q)
-
-    def project(i, carry):
-        acc = jnp.zeros((Q, LANES), F32)
-        for k in range(M):
-            acc = acc + dot(rows_all[k, rows_of(i), :KC], fce[k * KC:(k + 1) * KC, :])
-            acc = acc + dot(rows_all[k, rows_of(i), KC:], fcf[k * KC:(k + 1) * KC, :])
-        hpart[i] = acc
-        return carry
-
-    lax.fori_loop(0, X, project, 0)
+    hpart[...] = (dot(ef[0], fce[...]) + dot(ef[1], fcf[...])).reshape(2, X, H, LANES)
     for o in range(1, X):
         to = around(x, o, X)
-        ln.send(hpart.at[to], hrecv.at[x], (to, m, z), ("hidden", o))
+        ln.send(hpart.at[:, to], hrecv.at[x], (to, m, z), ("hidden", o))
+
+    def block_of(i):
+        return pl.ds(pl.multiple_of(i * LANES, LANES), LANES)
 
     def square(i, carry):
-        acc = jnp.zeros((Q, KC), F32)
+        acc = jnp.zeros((LANES, KC), F32)
         for k in range(M):
-            f = rows_all[k, rows_of(i), KC:].astype(F32)
+            f = ef[1, block_of(i), k * KC:(k + 1) * KC].astype(F32)
             acc = acc + f * f
         tq[x, i] = to_rows([jnp.sum(acc, axis=1, keepdims=True)])
         return carry
 
-    lax.fori_loop(0, X, square, 0)
+    lax.fori_loop(0, R // LANES, square, 0)
     for o in range(1, X):
         ln.send(tq.at[x], tq.at[x], (around(x, o, X), m, z), ("square", o))
 
-    hrecv[x] = hpart[x]
+    hrecv[x] = hpart[:, x]
     for o in range(1, X):
         ln.recv(hrecv.at[around(x, -o, X)], ("hidden", o))
     hsum = hrecv[0]
     for k in range(1, X):
         hsum = hsum + hrecv[k]
-    hmine[...] = hsum
+    hmine[...] = hsum.reshape(Q, LANES)
     ln.send(hmine, hblk, (y, x * C + c, z), "swap", when=off_diagonal)
 
     @pl.when(x == y)
     def _():
         hblk[...] = hmine[...]
-
-    for o in range(1, X):
-        ln.recv(tq.at[around(x, -o, X)], ("square", o))
 
     def normalize(i, carry):
         tile = tq[0, i]
@@ -378,159 +382,237 @@
             tile = tile + tq[k, i]
         scale = lax.rsqrt(to_columns(tile)[:, :1] / depth + eps_norm)
         for k in range(M):
-            f = rows_all[k, rows_of(i), KC:].astype(F32)
-            tnorm[rows_of(i), k * KC:(k + 1) * KC] = (f * scale * tgain_ref[:, k * KC:(k + 1) * KC]).astype(BF)
+            at = slice(k * KC, (k + 1) * KC)
+            f = ef[1, block_of(i), at].astype(F32)
+            tnorm[block_of(i), at] = (f * scale * tgain_ref[:, at]).astype(BF)
         return carry
 
+    def x_device(i):
+        return (i, m, z)
+
+    def logits(norm, into, h):
+        part = dot_last(norm[h * HALF:(h + 1) * HALF, :], head[...])
+        into[h] = part.reshape(X, H, vocab)
+
+    def logit_ring(name, h, part, up, down):
+        return Ring(
+            (name, h), x, X, x_device, lambda i: part.at[h, i], lambda k: up.at[h, k], lambda k: down.at[h, k]
+        )
+
+    target_rings = [logit_ring("tl", h, tl, tl_up, tl_down) for h in range(2)]
+    draft_rings = [logit_ring("dl", h, dl, dl_up, dl_down) for h in range(2)]
+    for o in range(1, X):
+        ln.recv(tq.at[around(x, -o, X)], ("square", o))
+    loads[4].wait()
+
+    def target_part(h):
+        lax.fori_loop(h * HALF // LANES, (h + 1) * HALF // LANES, normalize, 0)
+        logits(tnorm, tl, h)
+        target_rings[h].up(1)
+        target_rings[h].down(1)
+
+    target_part(0)
     ln.recv(hblk, "swap", when=off_diagonal)
     hid = hblk[...]
     second = add_up("dsq", to_rows([jnp.sum(hid * hid, axis=1, keepdims=True)]), 0, X * C, own_xc, xc_device)
-    lax.fori_loop(0, X, normalize, 0)
-    finish = second()
-    loads[4].wait()
-
-    def target_part(i):
-        tl[i] = dot_last(tnorm[rows_of(i), :], head[...])
-
-    def draft_part(i):
-        dl[i] = dot_last(dnorm[rows_of(i), :], head[...])
-
-    def x_device(i):
-        return (i, m, z)
-
-    draft_square = to_columns(finish())[:, :1]
+    target_part(1)
+    draft_square = to_columns(second()())[:, :1]
     dscale = lax.rsqrt(draft_square / depth + eps_norm)
-    block = c * Z + z
-    dgain = dgain_ref[pl.ds(block, 1), :]
+    dgain = dgain_ref[pl.ds(c * Z + z, 1), :]
 
     def norm_view(yy, cc, zz):
-        return dnorm.at[rows_of(yy), pl.ds(pl.multiple_of((cc * Z + zz) * LANES, LANES), LANES)]
-
-    norm_view(y, c, z)[...] = (hid * dscale * dgain).astype(BF)
-    target_sum = ring_sum("tl", x, X, x_device, lambda i: tl.at[i], tl_a, tl_b, target_part)
-    plane_gather("norm", norm_view)
-
-    draft_sum = ring_sum("dl", x, X, x_device, lambda i: dl.at[i], dl_a, dl_b, draft_part)
-    target_logit = target_sum()
-    draft_logit = draft_sum()
-
-    local = lax.broadcasted_iota(I32, (Q, 1), 0) + x * Q
-    packed = Z * (local % GROUP) + local // GROUP
-    labels = jnp.zeros((Q, 1), I32)
-    lane = lax.broadcasted_iota(I32, (Q, seq_len), 1)
-    for k in range(seqs):
-        inside = (packed >= start[k]) & (packed < start[k] + lengths_ref[k])
-        position = jnp.where(inside, offsets_ref[k] + packed - start[k], -1)
-        token = jnp.where(lane == position, tokens_ref[k:k + 1, :], 0)
-        labels = labels + jnp.sum(token, axis=1, keepdims=True)
-    column = lax.broadcasted_iota(I32, (Q, vocab), 1) + (m * Z + z) * vocab
-    is_label = column == labels
-    target_exp = jnp.exp(target_logit)
-    sums = to_rows([
-        jnp.sum(target_exp, axis=1, keepdims=True),
-        jnp.sum(target_exp * draft_logit, axis=1, keepdims=True),
-        jnp.sum(jnp.exp(draft_logit), axis=1, keepdims=True),
-        jnp.sum(jnp.where(is_label, draft_logit, 0.0), axis=1, keepdims=True),
-    ])
-    base = Z + X * C
-    sums = add_up("sums", sums, base, M, m, lambda g: (x, g, z))()()
-    columns = to_columns(sums)
-    target_lse = jnp.log(columns[:, 0:1])
-    draft_lse = jnp.log(columns[:, 2:3])
-    grad = (
-        (1.0 + 2.0 * z_weight * draft_lse) * jnp.exp(draft_logit - draft_lse)
-        - (1.0 - label_mix) * jnp.exp(target_logit - target_lse)
-        - label_mix * is_label.astype(F32)
-    )
-    lgrad[x] = grad.astype(BF)
-
-    v = lgrad.at[x]
-    ln.send(v, v, x_device(turn(x, 1, X)), ("lg", 1))
-    if X > 2:
-        ln.send(v, v, x_device(turn(x, -1, X)), ("lg", -1))
-
-    lse_row = jnp.log(sums[2:3])
-    row_loss = (
-        lse_row
-        - (1.0 - label_mix) * sums[1:2] / sums[0:1]
-        - label_mix * sums[3:4]
-        + z_weight * lse_row * lse_row
-    )
-    lossbuf[x] = jnp.broadcast_to(row_loss, (8, LANES))
+        columns = pl.ds(pl.multiple_of((cc * Z + zz) * LANES, LANES), LANES)
+        return dnorm.at[:, pl.ds(pl.multiple_of(yy * H, H), H), columns]
+
+    norm_view(y, c, z)[...] = (hid * dscale * dgain).astype(BF).reshape(2, H, LANES)
+    plane_gather("norm", norm_view, {1: lambda: target_rings[0].up(2), 3: lambda: target_rings[1].up(2)})
+
+    def draft_part(h):
+        part = dot_last(dnorm[h], head[...])
+        dl[h] = part.reshape(X, H, vocab)
+
+    draft_part(0)
+    draft_rings[0].up(1)
+    draft_rings[0].down(1)
+    draft_part(1)
+    draft_rings[1].up(1)
+
+    column = lax.broadcasted_iota(I32, (H, vocab), 1) + (m * Z + z) * vocab
+
+    def labels_of(h):
+        local = lax.broadcasted_iota(I32, (H, 1), 0) + h * HALF + x * H
+        packed = Z * (local % GROUP) + local // GROUP
+        labels = jnp.zeros((H, 1), I32)
+        lane = lax.broadcasted_iota(I32, (H, seq_len), 1)
+        for k in range(seqs):
+            inside = (packed >= start[k]) & (packed < start[k] + lengths_ref[k])
+            position = jnp.where(inside, offsets_ref[k] + packed - start[k], -1)
+            token = jnp.where(lane == position, tokens_ref[k:k + 1, :], 0)
+            labels = labels + jnp.sum(token, axis=1, keepdims=True)
+        return labels
+
+    labels = [labels_of(h) for h in range(2)]
+
+    target_total = []
+    for h in range(2):
+        target_logit = target_rings[h].finish()
+        tl[h, x] = target_logit
+        target_total.append(jnp.sum(jnp.exp(target_logit), axis=1, keepdims=True))
+    draft_rings[0].up(2)
+    draft_rings[1].down(1)
+    draft_rings[1].up(2)
+
+    def softmax_sums(h):
+        draft_logit = draft_rings[h].finish()
+        dl[h, x] = draft_logit
+        sums = [
+            target_total[h],
+            jnp.sum(jnp.exp(tl[h, x]) * draft_logit, axis=1, keepdims=True),
+            jnp.sum(jnp.exp(draft_logit), axis=1, keepdims=True),
+            jnp.sum(jnp.where(column == labels[h], draft_logit, 0.0), axis=1, keepdims=True),
+        ]
+        tile = to_rows([jnp.concatenate([column_sum] * (LANES // H), axis=0) for column_sum in sums])
+        base = Z + X * C + h * (Z + M)
+        return add_up(("sums", h), tile, base, M, m, lambda g: (x, g, z))
+
+    def logit_grad(h, sums):
+        columns = to_columns(sums)[:H]
+        target_lse = jnp.log(columns[:, 0:1])
+        draft_lse = jnp.log(columns[:, 2:3])
+        grad = (
+            (1.0 + 2.0 * z_weight * draft_lse) * jnp.exp(dl[h, x] - draft_lse)
+            - (1.0 - label_mix) * jnp.exp(tl[h, x] - target_lse)
+            - jnp.where(column == labels[h], label_mix, 0.0)
+        )
+        lgrad[h, x] = grad.astype(BF)
+        v = lgrad.at[h, x]
+        ln.send(v, v, x_device(turn(x, 1, X)), ("lg", h, 1))
+        if X > 2:
+            ln.send(v, v, x_device(turn(x, -1, X)), ("lg", h, -1))
+
+    def row_loss(sums):
+        lse = jnp.log(sums[2:3])
+        return (
+            lse
+            - (1.0 - label_mix) * sums[1:2] / sums[0:1]
+            - label_mix * sums[3:4]
+            + z_weight * lse * lse
+        )
+
+    def grad_pass(h):
+        v = lgrad.at[h, turn(x, -1, X)]
+        ln.recv(v, ("lg", h, 1))
+        if X > 2:
+            ln.send(v, v, x_device(turn(x, 1, X)), ("lg", h, 2))
+
+    def grad_arrived(h):
+        if X > 2:
+            ln.recv(lgrad.at[h, turn(x, 1, X)], ("lg", h, -1))
+            ln.recv(lgrad.at[h, turn(x, 2, X)], ("lg", h, 2))
+
+    def grad_part(h, half):
+        part = dot(lgrad[h].reshape(HALF, vocab), head[:, pl.ds(pl.multiple_of(half * side, side), side)])
+        dg[h, half] = part.reshape(Y, H, side)
+
+    def other_half(h):
+        grad_part(h, 1 - c)
+        ln.send(dg.at[h, 1 - c], dg_in.at[h], sibling, ("dgc", h))
+
+    def own_half(h):
+        grad_part(h, c)
+        ln.recv(dg_in.at[h], ("dgc", h))
+        dg[h, c] += dg_in[h]
+
+    y_rings = [
+        Ring(("dgy", h), y, Y, lambda i: (x, i * C + c, z), lambda i, h=h: dg.at[h, c, i],
+             lambda k, h=h: dg_up.at[h, k], lambda k, h=h: dg_down.at[h, k])
+        for h in range(2)
+    ]
+    z_rings = [
+        Ring(("dgz", h), z, Z, lambda i: (x, m, i), lambda i, h=h: dz.at[h, i],
+             lambda k, h=h: dz_up.at[h, k], lambda k, h=h: dz_down.at[h, k])
+        for h in range(2)
+    ]
+
+    def to_z(h):
+        summed = y_rings[h].finish()
+        for k in range(Z):
+            dz[h, k] = summed[:, k * LANES:(k + 1) * LANES]
+        z_step(h, 1)
+
+    def z_step(h, k):
+        z_rings[h].up(k)
+        z_rings[h].down(k)
+
+    second_0 = softmax_sums(0)
+    finish_0 = second_0()
+    second_1 = softmax_sums(1)
+    sums_0 = finish_0()
+    logit_grad(0, sums_0)
+    finish_1 = second_1()
+    grad_pass(0)
+    sums_1 = finish_1()
+    logit_grad(1, sums_1)
+    grad_arrived(0)
+    other_half(0)
+    lossbuf[x] = jnp.broadcast_to(row_loss(sums_0) + row_loss(sums_1), (8, LANES))
     for o in range(1, X):
         ln.send(lossbuf.at[x], lossbuf.at[x], (around(x, o, X), m, z), ("loss", o))
-
-    v = lgrad.at[turn(x, -1, X)]
-    ln.recv(v, ("lg", 1))
-    if X > 2:
-        ln.send(v, v, x_device(turn(x, 1, X)), ("lg", 2))
-        ln.recv(lgrad.at[turn(x, 1, X)], ("lg", -1))
-        ln.recv(lgrad.at[turn(x, 2, X)], ("lg", 2))
-
-    side = Z * LANES
-
-    def grad_part(half, i):
-        dg[half, i] = dot(lgrad[i], head[:, pl.ds(pl.multiple_of(half * side, side), side)])
-
-    sibling = (x, y * C + 1 - c, z)
-    for o in ([2, 1, -1, 0] if Y > 2 else [1, 0]):
-        i = turn(y, o, Y)
-        grad_part(1 - c, i)
-        ln.send(dg.at[1 - c, i], dg_in.at[i], sibling, ("dgc", -o % Y))
-
-    def own_part(i, o):
-        grad_part(c, i)
-        ln.recv(dg_in.at[i], ("dgc", o % Y))
-        dg[c, i] += dg_in[i]
-
-    todo = iter([2, -1, 1, 0] if Y > 2 else [1, 0])
-    summed = ring_sum(
-        "dgy", y, Y, lambda i: (x, i * C + c, z), lambda i: dg.at[c, i], dg_a, dg_b, lambda i: own_part(i, next(todo))
-    )()
-    for k in range(Z):
-        dz[k] = summed[:, k * LANES:(k + 1) * LANES]
-    dgrad = ring_sum("dgz", z, Z, lambda i: (x, m, i), lambda i: dz.at[i], dz_a, dz_b, lambda i: None)()
+    own_half(0)
+    y_rings[0].up(1)
+    y_rings[0].down(1)
+    grad_pass(1)
+    grad_arrived(1)
+    other_half(1)
+    own_half(1)
+    y_rings[0].up(2)
+    y_rings[1].up(1)
+    y_rings[1].down(1)
+    to_z(0)
+    z_step(0, 2)
+    y_rings[1].up(2)
+    z_step(0, 3)
+    z_step(0, 4)
+    to_z(1)
+    z_step(1, 2)
+    dgrad_0 = z_rings[0].finish()
+    z_step(1, 3)
+    z_step(1, 4)
+    dgrad = jnp.concatenate([dgrad_0, z_rings[1].finish()], axis=0)
 
     upstream = dgrad * dgain
     hid = hblk[...]
-    base = base + Z + M
-    inner = add_up("inner", to_rows([jnp.sum(hid * upstream, axis=1, keepdims=True)]), base, X * C, own_xc, xc_device)()()
-    inner = to_columns(inner)[:, :1]
-    hgrad = (dscale * upstream - hid * (dscale * dscale * dscale * inner / depth)).astype(BF)
+    base = Z + X * C + 2 * (Z + M)
+    inner = to_rows([jnp.sum(hid * upstream, axis=1, keepdims=True)])
+    inner = to_columns(add_up("inner", inner, base, X * C, own_xc, xc_device)()())[:, :1]
+    hgrad = (dscale * upstream - hid * (dscale * dscale * dscale * inner / depth)).astype(BF).reshape(2, H, LANES)
     hg_out[...] = hgrad
-    names = [("hg", q) for q in range(Y)]
     first_name = len(ln.tags)
-    for name in names:
-        ln.tag(name)
+    for q in range(Y):
+        ln.tag(("hg", q))
     for o in range(X):
         ln.send(
-            hg_out, hg.at[y], (around(x, o, X), x * C + c, z), None,
+            hg_out, hg.at[:, y], (around(x, o, X), x * C + c, z), None,
             when=off_diagonal if o == 0 else None, recv_sem=recv_sems.at[first_name + y],
         )
 
     @pl.when(x == y)
     def _():
-        hg[y] = hgrad
+        hg[:, y] = hgrad
 
     for o in range(1, X):
         ln.recv(lossbuf.at[around(x, -o, X)], ("loss", o))
     part = lossbuf[0]
     for k in range(1, X):
         part = part + lossbuf[k]
-    loss_ref[0, 0] = jnp.sum(part[:1]) / R
+    loss_ref[0, 0] = jnp.sum(part[:1]) / (R * (LANES // H))
 
     for o in range(Y):
         q = around(y, o, Y)
-        ln.recv(hg.at[q], None, when=off_diagonal if o == 0 else None, recv_sem=recv_sems.at[first_name + q])
+        ln.recv(hg.at[:, q], None, when=off_diagonal if o == 0 else None, recv_sem=recv_sems.at[first_name + q])
     block_grad = hg[...].reshape(R, LANES)
-
-    def outer(k, carry):
-        at = pl.ds(pl.multiple_of(k * KC, KC), KC)
-        ge_ref[at, :] = dot_first(rows_all[k, :, :KC], block_grad)
-        gf_ref[at, :] = dot_first(rows_all[k, :, KC:], block_grad)
-        return carry
-
-    lax.fori_loop(0, M, outer, 0)
+    ge_ref[...] = dot_first(ef[0], block_grad)
+    gf_ref[...] = dot_first(ef[1], block_grad)
     ln.finish()
 
 
@@ -563,20 +645,21 @@
     halfz = Z // 2
     side = Z * LANES
     V = pltpu.VMEM
+    H = Q // 2
     scratch = [
         V((seq_len, KC), BF), V((seq_len, KC), BF), V((vocab, width), BF), V((width, LANES), BF), V((width, LANES), BF),
-        V((Z * SL, 2 * KC), BF), V((Z * SL, 2 * KC), BF), V((M, R, 2 * KC), BF),
-        V((X, Q, LANES), F32), V((X, Q, LANES), F32), V((Q, LANES), F32), V((Q, LANES), F32),
-        V((X, X, 8, LANES), F32), V((R, width), BF), V((R, width), BF),
-        V((X, Q, vocab), F32), V((half, Q, vocab), F32), V((rest, Q, vocab), F32),
-        V((X, Q, vocab), F32), V((half, Q, vocab), F32), V((rest, Q, vocab), F32),
-        V((3 * Z + 2 * X * C + M, 8, LANES), F32), V((X, 8, LANES), F32),
-        V((X, Q, vocab), BF),
-        V((C, Y, Q, side), F32), V((Y, Q, side), F32),
-        V((halfy, Q, side), F32), V((max(1, halfy - 1), Q, side), F32),
-        V((Z, Q, LANES), F32), V((halfz, Q, LANES), F32), V((max(1, halfz - 1), Q, LANES), F32),
-        V((Q, LANES), BF), V((Y, Q, LANES), BF),
-        pltpu.SemaphoreType.DMA((224,)), pltpu.SemaphoreType.DMA((224,)), pltpu.SemaphoreType.DMA((5,)),
+        V((Z * SL, 2 * KC), BF), V((Z * SL, 2 * KC), BF), V((2, R, width), BF),
+        V((2, X, H, LANES), F32), V((X, 2, H, LANES), F32), V((Q, LANES), F32), V((Q, LANES), F32),
+        V((X, R // LANES, 8, LANES), F32), V((R, width), BF), V((2, R // 2, width), BF),
+        V((2, X, H, vocab), F32), V((2, half, H, vocab), F32), V((2, rest, H, vocab), F32),
+        V((2, X, H, vocab), F32), V((2, half, H, vocab), F32), V((2, rest, H, vocab), F32),
+        V((4 * Z + 2 * X * C + 2 * M, 8, LANES), F32), V((X, 8, LANES), F32),
+        V((2, X, H, vocab), BF),
+        V((2, C, Y, H, side), F32), V((2, Y, H, side), F32),
+        V((2, halfy, H, side), F32), V((2, max(1, halfy - 1), H, side), F32),
+        V((2, Z, H, LANES), F32), V((2, halfz, H, LANES), F32), V((2, max(1, halfz - 1), H, LANES), F32),
+        V((2, H, LANES), BF), V((2, Y, H, LANES), BF),
+        pltpu.SemaphoreType.DMA((256,)), pltpu.SemaphoreType.DMA((256,)), pltpu.SemaphoreType.DMA((5,)),
     ]
     smem = pl.BlockSpec(memory_space=pltpu.SMEM)
     vmem = pl.BlockSpec(memory_space=pltpu.VMEM)

time: 211 us -> 190 us (0.900); the launches traced: 209 us -> 190 us
  Pallas kernels: 202 us -> 183 us
    pallas_call x1, Pallas kernels: 202 us -> 183 us  [on_device(): pl.pallas_call(functools.partial(kernel, (X, M, Z, R)), out_shape=(jax.Sh...]
where the time goes in v2:
time: 190 us
  Pallas kernels  183 us (96%)
  local copies, waits for them, and re-layouts  4.52 us (2%)
  between operations  2.38 us (1%)
    pallas_call x1, Pallas kernels, on_device(): pl.pallas_call(functools.partial(kernel, (X, M, Z, R)), out_shape=(jax.Sh...  183 us
    unnamed x2, local copies, waits for them, and re-layouts  4.52 us

profile of v2, /device:TPU:1, one launch (start us, length us, event | category | flops | bytes accessed | tf_op | source)
XLA Modules:
  0.0 189.9 jit_solution(9557017862402682863)
XLA Ops:
  0.6 183.0 %shard_map.121 = (f32[1,1]{1,0:T(1,128)}, f32[2048,128]{1,0:T(8,128)}, f32[2048,128]{1,0:T(8,128)}) custom-call(s32[8]{0:T(128)} %lengths_ref.1, s32[8]{0:T(128)} %offsets_ref.1, s32[8,256]{1,0:T(8,128)} %tokens_ref.1, f32[1,2048]{1,0:T(1,128)} %bitcast.3, f32[16,128]{1,0:T(8,128)} %bitcast.4, bf16[1,256,2048]{2,1,0:T(8,128)(2,1)} %feat_hbm.1, ...), custom_call_target="tpu_custom_call" | custom-call | flops 7500000256 | bytes 10000000 | tf_op jit(solution)/shard_map/pallas_call | solution.py:667
  184.3 2.3 %copy.17 = f32[2048,128]{1,0:T(8,128)} copy(f32[2048,128]{1,0:T(8,128)} %get-tuple-element.13) | data formatting | bytes 2097152
  186.6 2.3 %copy.18 = f32[2048,128]{1,0:T(8,128)} copy(f32[2048,128]{1,0:T(8,128)} %get-tuple-element.14) | data formatting | bytes 2097152

commit v3 on v2

--- a/solution.py
+++ b/solution.py
@@ -92,11 +92,12 @@
     sizes,
     lengths_ref, offsets_ref, tokens_ref, tgain_ref, dgain_ref,
     feat_hbm, emb_hbm, head_hbm, fce_hbm, fcf_hbm,
-    loss_ref, ge_ref, gf_ref,
+    loss_ref, hg_ref, ef_hbm,
     ebuf, fbuf, head, fce, fcf, pk, rk, ef,
     hpart, hrecv, hmine, hblk, tq, tnorm, dnorm,
-    tl, tl_up, tl_down, dl, dl_up, dl_down, arbuf, lossbuf,
-    lgrad, dg, dg_in, dg_up, dg_down, dz, dz_up, dz_down, hg_out, hg,
+    tl, tl_up, tl_down, dl, dl_up, dl_down, arbuf, lossbuf, inner_out,
+    lgrad, dg, dg_in, dg_up, dg_down, dz, dz_up, dz_down,
+    zf_up, zf_down, dy, dy_up, dy_down, hg_out, hg,
     send_sems, recv_sems, local_sems,
 ):
     X, M, Z, R = sizes
@@ -149,15 +150,13 @@
         g = around(own_xc, o, X * C)
         greet((g // C, y * C + g % C, z))
     off_diagonal = x != y
-    pl.when(off_diagonal)(lambda: greet((y, x * C + c, z)))
-    for o in range(Y):
-        q = around(y, o, Y)
+    for o in range(M):
         if o == 0:
-            pl.when(off_diagonal)(lambda q=q: greet((y, q * C + c, z)))
+            pl.when(off_diagonal)(lambda: greet((y, m, z)))
         else:
-            greet((y, q * C + c, z))
-    steady = (Z - 1) + (M - 1) + (X * C - 1) + (X - 1)
-    pl.semaphore_wait(barrier, steady + 2 * off_diagonal.astype(I32))
+            greet((y, around(m, o, M), z))
+    steady = (Z - 1) + (M - 1) + (X * C - 1) + (X * C - 1)
+    pl.semaphore_wait(barrier, steady + off_diagonal.astype(I32))
 
     start, total = [], jnp.int32(0)
     for k in range(seqs):
@@ -263,12 +262,57 @@
             if 0 <= k - 2 <= half:
                 for o in waves[k - 2]:
                     from_y2(o)
-            if beside and k in beside:
-                beside[k]()
+            if beside:
+                beside(k)
         for wave in waves:
             for o in wave:
                 for a in range(Y):
                     ln.recv(view(at_y(a), 1 - c, at_z(o)), (name, "core", a % Y, o % Z))
+
+    def plane_gather_y(name, piece, block):
+        half = Z // 2
+        halfy = Y // 2
+
+        def y_device(a):
+            return (x, turn(y, a, Y) * C + c, z)
+
+        v = piece(y)
+        ln.send(v, v, y_device(1), (name, "y+"))
+        if halfy > 1:
+            ln.send(v, v, y_device(-1), (name, "y-"))
+        yield
+        v = piece(turn(y, -1, Y))
+        ln.recv(v, (name, "y+"))
+        if halfy > 1:
+            ln.send(v, v, y_device(1), (name, "y2"))
+            ln.recv(piece(turn(y, 1, Y)), (name, "y-"))
+            yield
+            ln.recv(piece(turn(y, 2, Y)), (name, "y2"))
+
+        def z_pass(k):
+            v = block(c, turn(z, -(k - 1), Z))
+            ln.send(v, v, (x, m, turn(z, 1, Z)), (name, "z+", k))
+            if k < half:
+                v = block(c, turn(z, k - 1, Z))
+                ln.send(v, v, (x, m, turn(z, -1, Z)), (name, "z-", k))
+
+        def across(o):
+            v = block(c, turn(z, o, Z))
+            ln.send(v, v, sibling, (name, "core", -o % Z))
+
+        z_pass(1)
+        across(0)
+        for k in range(1, half + 1):
+            yield
+            ln.recv(block(c, turn(z, -k, Z)), (name, "z+", k))
+            if k < half:
+                ln.recv(block(c, turn(z, k, Z)), (name, "z-", k))
+                z_pass(k + 1)
+                across(k)
+            across(-k)
+        yield
+        for o in range(Z):
+            ln.recv(block(1 - c, turn(z, o, Z)), (name, "core", o))
 
     class Ring:
         def __init__(self, name, me, n, device, chunk, up, down):
@@ -341,6 +385,9 @@
 
     plane_gather("rows", rows_view)
 
+    rows_out = pltpu.make_async_copy(ef, ef_hbm, local_sems.at[5])
+    rows_out.start()
+
     loads[2].wait()
     loads[3].wait()
     hpart[...] = (dot(ef[0], fce[...]) + dot(ef[1], fcf[...])).reshape(2, X, H, LANES)
@@ -420,12 +467,26 @@
     dscale = lax.rsqrt(draft_square / depth + eps_norm)
     dgain = dgain_ref[pl.ds(c * Z + z, 1), :]
 
-    def norm_view(yy, cc, zz):
-        columns = pl.ds(pl.multiple_of((cc * Z + zz) * LANES, LANES), LANES)
-        return dnorm.at[:, pl.ds(pl.multiple_of(yy * H, H), H), columns]
-
-    norm_view(y, c, z)[...] = (hid * dscale * dgain).astype(BF).reshape(2, H, LANES)
-    plane_gather("norm", norm_view, {1: lambda: target_rings[0].up(2), 3: lambda: target_rings[1].up(2)})
+    def norm_columns(cc, zz):
+        return pl.ds(pl.multiple_of((cc * Z + zz) * LANES, LANES), LANES)
+
+    def norm_view(h, yy, cc, zz):
+        return dnorm.at[h, pl.ds(pl.multiple_of(yy * H, H), H), norm_columns(cc, zz)]
+
+    norm = (hid * dscale * dgain).astype(BF)
+    norm_view(0, y, c, z)[...] = norm[:H]
+    norm_view(1, y, c, z)[...] = norm[H:]
+    second_gather = plane_gather_y(
+        "norm1", lambda yy: norm_view(1, yy, c, z), lambda cc, zz: dnorm.at[1, :, norm_columns(cc, zz)]
+    )
+    next(second_gather)
+
+    def beside(k):
+        next(second_gather, None)
+        if k in (2, 4):
+            target_rings[k // 2 - 1].up(2)
+
+    plane_gather("norm0", functools.partial(norm_view, 0), beside)
 
     def draft_part(h):
         part = dot_last(dnorm[h], head[...])
@@ -434,6 +495,8 @@
     draft_part(0)
     draft_rings[0].up(1)
     draft_rings[0].down(1)
+    for _ in second_gather:
+        pass
     draft_part(1)
     draft_rings[1].up(1)
 
@@ -484,11 +547,58 @@
             - (1.0 - label_mix) * jnp.exp(tl[h, x] - target_lse)
             - jnp.where(column == labels[h], label_mix, 0.0)
         )
-        lgrad[h, x] = grad.astype(BF)
+        grad = grad.astype(BF)
+        lgrad[h, x] = grad
         v = lgrad.at[h, x]
         ln.send(v, v, x_device(turn(x, 1, X)), ("lg", h, 1))
         if X > 2:
             ln.send(v, v, x_device(turn(x, -1, X)), ("lg", h, -1))
+        return jnp.sum(grad.astype(F32) * dl[h, x], axis=1, keepdims=True)
+
+    inner_base = Z + X * C + 2 * (Z + M)
+
+    def inner_first(columns):
+        arbuf[inner_base + z] = to_rows([jnp.concatenate(columns, axis=0)])
+        for o in range(1, Z):
+            v = arbuf.at[inner_base + z]
+            ln.send(v, v, (x, m, around(z, o, Z)), ("inner", o))
+
+    def inner_second():
+        for o in range(1, Z):
+            ln.recv(arbuf.at[inner_base + around(z, -o, Z)], ("inner", o))
+        part = arbuf[inner_base]
+        for k in range(1, Z):
+            part = part + arbuf[inner_base + k]
+        inner_out[...] = part
+        first_name = len(ln.tags)
+        for k in range(M):
+            ln.tag(("inner row", k))
+        for o in range(X):
+            for side_core in range(C):
+                own = o == 0 and side_core == 0
+                ln.send(
+                    inner_out, arbuf.at[inner_base + Z + m],
+                    (around(x, o, X), x * C + (c + side_core) % C, z), ("inner to", o, side_core),
+                    when=off_diagonal if own else None, recv_sem=recv_sems.at[first_name + m],
+                )
+
+        @pl.when(x == y)
+        def _():
+            arbuf[inner_base + Z + m] = inner_out[...]
+
+        return first_name
+
+    def inner_third(first_name):
+        for o in range(M):
+            k = around(m, o, M)
+            ln.recv(
+                arbuf.at[inner_base + Z + k], ("inner to", o // C, o % C),
+                when=off_diagonal if o == 0 else None, recv_sem=recv_sems.at[first_name + k],
+            )
+        part = arbuf[inner_base + Z]
+        for k in range(1, M):
+            part = part + arbuf[inner_base + Z + k]
+        return to_columns(part)[:, :1]
 
     def row_loss(sums):
         lse = jnp.log(sums[2:3])
@@ -523,69 +633,69 @@
         ln.recv(dg_in.at[h], ("dgc", h))
         dg[h, c] += dg_in[h]
 
-    y_rings = [
-        Ring(("dgy", h), y, Y, lambda i: (x, i * C + c, z), lambda i, h=h: dg.at[h, c, i],
-             lambda k, h=h: dg_up.at[h, k], lambda k, h=h: dg_down.at[h, k])
-        for h in range(2)
-    ]
-    z_rings = [
-        Ring(("dgz", h), z, Z, lambda i: (x, m, i), lambda i, h=h: dz.at[h, i],
-             lambda k, h=h: dz_up.at[h, k], lambda k, h=h: dz_down.at[h, k])
-        for h in range(2)
-    ]
-
-    def to_z(h):
-        summed = y_rings[h].finish()
-        for k in range(Z):
-            dz[h, k] = summed[:, k * LANES:(k + 1) * LANES]
-        z_step(h, 1)
-
-    def z_step(h, k):
-        z_rings[h].up(k)
-        z_rings[h].down(k)
+    ring_z0 = Ring(
+        "z0", z, Z, lambda i: (x, m, i),
+        lambda i: dg.at[0, c, :, :, pl.ds(pl.multiple_of(i * LANES, LANES), LANES)],
+        lambda k: zf_up.at[k], lambda k: zf_down.at[k],
+    )
+    ring_y0 = Ring(
+        "y0", y, Y, lambda i: (x, i * C + c, z), lambda i: dy.at[i], lambda k: dy_up.at[k], lambda k: dy_down.at[k]
+    )
+    ring_y1 = Ring(
+        "y1", y, Y, lambda i: (x, i * C + c, z), lambda i: dg.at[1, c, i], lambda k: dg_up.at[k], lambda k: dg_down.at[k]
+    )
+    ring_z1 = Ring(
+        "z1", z, Z, lambda i: (x, m, i), lambda i: dz.at[i], lambda k: dz_up.at[k], lambda k: dz_down.at[k]
+    )
+
+    def step(ring, k):
+        ring.up(k)
+        ring.down(k)
 
     second_0 = softmax_sums(0)
     finish_0 = second_0()
     second_1 = softmax_sums(1)
     sums_0 = finish_0()
-    logit_grad(0, sums_0)
+    inner_0 = logit_grad(0, sums_0)
     finish_1 = second_1()
     grad_pass(0)
     sums_1 = finish_1()
-    logit_grad(1, sums_1)
+    inner_1 = logit_grad(1, sums_1)
     grad_arrived(0)
     other_half(0)
+    inner_first([inner_0, inner_1])
+    own_half(0)
+    step(ring_z0, 1)
+    grad_pass(1)
+    grad_arrived(1)
+    other_half(1)
+    inner_name = inner_second()
+    own_half(1)
+    step(ring_y1, 1)
+    step(ring_z0, 2)
     lossbuf[x] = jnp.broadcast_to(row_loss(sums_0) + row_loss(sums_1), (8, LANES))
     for o in range(1, X):
         ln.send(lossbuf.at[x], lossbuf.at[x], (around(x, o, X), m, z), ("loss", o))
-    own_half(0)
-    y_rings[0].up(1)
-    y_rings[0].down(1)
-    grad_pass(1)
-    grad_arrived(1)
-    other_half(1)
-    own_half(1)
-    y_rings[0].up(2)
-    y_rings[1].up(1)
-    y_rings[1].down(1)
-    to_z(0)
-    z_step(0, 2)
-    y_rings[1].up(2)
-    z_step(0, 3)
-    z_step(0, 4)
-    to_z(1)
-    z_step(1, 2)
-    dgrad_0 = z_rings[0].finish()
-    z_step(1, 3)
-    z_step(1, 4)
-    dgrad = jnp.concatenate([dgrad_0, z_rings[1].finish()], axis=0)
+    inner = inner_third(inner_name)
+    ring_y1.up(2)
+    step(ring_z0, 3)
+    step(ring_z0, 4)
+    summed = ring_y1.finish()
+    for k in range(Z):
+        dz[k] = summed[:, k * LANES:(k + 1) * LANES]
+    step(ring_z1, 1)
+    dy[...] = ring_z0.finish()
+    step(ring_y0, 1)
+    step(ring_z1, 2)
+    ring_y0.up(2)
+    step(ring_z1, 3)
+    step(ring_z1, 4)
+    dgrad_0 = ring_y0.finish()
+    dgrad = jnp.concatenate([dgrad_0, ring_z1.finish()], axis=0)
 
     upstream = dgrad * dgain
     hid = hblk[...]
-    base = Z + X * C + 2 * (Z + M)
-    inner = to_rows([jnp.sum(hid * upstream, axis=1, keepdims=True)])
-    inner = to_columns(add_up("inner", inner, base, X * C, own_xc, xc_device)()())[:, :1]
-    hgrad = (dscale * upstream - hid * (dscale * dscale * dscale * inner / depth)).astype(BF).reshape(2, H, LANES)
+    hgrad = (dscale * upstream - hid * (dscale * dscale * inner / depth)).astype(BF).reshape(2, H, LANES)
     hg_out[...] = hgrad
     first_name = len(ln.tags)
     for q in range(Y):
@@ -610,10 +720,14 @@
     for o in range(Y):
         q = around(y, o, Y)
         ln.recv(hg.at[:, q], None, when=off_diagonal if o == 0 else None, recv_sem=recv_sems.at[first_name + q])
-    block_grad = hg[...].reshape(R, LANES)
-    ge_ref[...] = dot_first(ef[0], block_grad)
-    gf_ref[...] = dot_first(ef[1], block_grad)
+    hg_ref[...] = hg[...].reshape(R, LANES)
+    rows_out.wait()
     ln.finish()
+
+
+def outer(ef_ref, hg_ref, ge_ref, gf_ref):
+    ge_ref[...] = dot_first(ef_ref[0], hg_ref[...])
+    gf_ref[...] = dot_first(ef_ref[1], hg_ref[...])
 
 
 def on_device(
@@ -643,6 +757,7 @@
     rest = max(1, half - 1)
     halfy = Y // 2
     halfz = Z // 2
+    resty, restz = max(1, halfy - 1), max(1, halfz - 1)
     side = Z * LANES
     V = pltpu.VMEM
     H = Q // 2
@@ -653,26 +768,28 @@
         V((X, R // LANES, 8, LANES), F32), V((R, width), BF), V((2, R // 2, width), BF),
         V((2, X, H, vocab), F32), V((2, half, H, vocab), F32), V((2, rest, H, vocab), F32),
         V((2, X, H, vocab), F32), V((2, half, H, vocab), F32), V((2, rest, H, vocab), F32),
-        V((4 * Z + 2 * X * C + 2 * M, 8, LANES), F32), V((X, 8, LANES), F32),
+        V((4 * Z + X * C + 3 * M, 8, LANES), F32), V((X, 8, LANES), F32), V((8, LANES), F32),
         V((2, X, H, vocab), BF),
         V((2, C, Y, H, side), F32), V((2, Y, H, side), F32),
-        V((2, halfy, H, side), F32), V((2, max(1, halfy - 1), H, side), F32),
-        V((2, Z, H, LANES), F32), V((2, halfz, H, LANES), F32), V((2, max(1, halfz - 1), H, LANES), F32),
+        V((halfy, H, side), F32), V((resty, H, side), F32),
+        V((Z, H, LANES), F32), V((halfz, H, LANES), F32), V((restz, H, LANES), F32),
+        V((halfz, Y, H, LANES), F32), V((restz, Y, H, LANES), F32),
+        V((Y, H, LANES), F32), V((halfy, H, LANES), F32), V((resty, H, LANES), F32),
         V((2, H, LANES), BF), V((2, Y, H, LANES), BF),
-        pltpu.SemaphoreType.DMA((256,)), pltpu.SemaphoreType.DMA((256,)), pltpu.SemaphoreType.DMA((5,)),
+        pltpu.SemaphoreType.DMA((288,)), pltpu.SemaphoreType.DMA((288,)), pltpu.SemaphoreType.DMA((6,)),
     ]
     smem = pl.BlockSpec(memory_space=pltpu.SMEM)
     vmem = pl.BlockSpec(memory_space=pltpu.VMEM)
     hbm = pl.BlockSpec(memory_space=pl.ANY)
-    loss, grad_embed, grad_feature = pl.pallas_call(
+    loss, block_grad, rows = pl.pallas_call(
         functools.partial(kernel, (X, M, Z, R)),
         out_shape=(
             jax.ShapeDtypeStruct((1, 1), F32),
-            jax.ShapeDtypeStruct((width, LANES), F32),
-            jax.ShapeDtypeStruct((width, LANES), F32),
+            jax.ShapeDtypeStruct((R, LANES), BF),
+            jax.ShapeDtypeStruct((2, R, width), BF),
         ),
         in_specs=[smem, smem, vmem, vmem, vmem, hbm, hbm, hbm, hbm, hbm],
-        out_specs=(smem, vmem, vmem),
+        out_specs=(smem, vmem, hbm),
         scratch_shapes=scratch,
         compiler_params=pltpu.CompilerParams(
             collective_id=0, has_side_effects=True, vmem_limit_bytes=56 * 1024 * 1024
@@ -682,6 +799,18 @@
         lengths, offsets, token_ids, target_gain.reshape(1, width), draft_gain.reshape(width // LANES, LANES),
         target_hidden, embeds, head, fc_embed, fc_feature,
     )
+    tile = min(512, width)
+    grad_embed, grad_feature = pl.pallas_call(
+        outer,
+        grid=(width // tile,),
+        out_shape=(jax.ShapeDtypeStruct((width, LANES), F32), jax.ShapeDtypeStruct((width, LANES), F32)),
+        in_specs=[
+            pl.BlockSpec((2, R, tile), lambda i: (0, 0, i)),
+            pl.BlockSpec((R, LANES), lambda i: (0, 0)),
+        ],
+        out_specs=(pl.BlockSpec((tile, LANES), lambda i: (i, 0)), pl.BlockSpec((tile, LANES), lambda i: (i, 0))),
+        compiler_params=pltpu.CompilerParams(vmem_limit_bytes=32 * 1024 * 1024),
+    )(rows, block_grad)
     return loss[0, 0], grad_embed, grad_feature
 
 

time: 190 us -> 178 us (0.937); the launches traced: 190 us -> 175 us
  Pallas kernels: 183 us -> 169 us
    pallas_call x1, Pallas kernels: 183 us -> 166 us  [on_device(): pl.pallas_call(functools.partial(kernel, (X, M, Z, R)), out_shape=(jax.Sh...]
    pallas_call x0 -> x1, Pallas kernels: none -> 3.32 us  [on_device(): pl.pallas_call(outer, grid=(width // tile,), out_shape=(jax.ShapeDtypeStr...]
    unnamed x2 -> x4, local copies, waits for them, and re-layouts: 4.52 us -> 3.08 us
where the time goes in v3:
time: 178 us; the launch traced here: 175 us
  Pallas kernels  169 us (95%)
  local copies, waits for them, and re-layouts  3.08 us (2%)
  between operations  2.36 us (1%)
    pallas_call x1, Pallas kernels, on_device(): pl.pallas_call(functools.partial(kernel, (X, M, Z, R)), out_shape=(jax.Sh...  166 us

profile of v3, /device:TPU:1, one launch (start us, length us, event | category | flops | bytes accessed | tf_op | source)
XLA Modules:
  0.0 174.7 jit_solution(4315329714423027370)
XLA Ops:
  0.6 165.9 %shard_map.121 = (f32[1,1]{1,0:T(1,128)}, bf16[512,128]{1,0:T(8,128)(2,1)}, bf16[2,512,2048]{2,1,0:T(8,128)(2,1)}) custom-call(s32[8]{0:T(128)} %lengths_ref.1, s32[8]{0:T(128)} %offsets_ref.1, s32[8,256]{1,0:T(8,128)} %tokens_ref.1, f32[1,2048]{1,0:T(1,128)} %bitcast.3, f32[16,128]{1,0:T(8,128)} %bitcast.4, bf16[1,256,2048]{2,1,0:T(8,128)(2,1)} %feat_hbm.1, ...), custom_call_target="tpu_custom_call" | custom-call | flops 7500000256 | bytes 10000000 | tf_op jit(solution)/shard_map/pallas_call | solution.py:784
  166.6 0.0 copy-start
  166.6 2.2 %copy-done = bf16[2,512,2048]{2,1,0:T(8,128)(2,1)S(1)} copy-done((bf16[2,512,2048]{2,1,0:T(8,128)(2,1)S(1)}, bf16[2,512,2048]{2,1,0:T(8,128)(2,1)}, u32[]{:S(2)}) %copy-start) | copy-done | bytes 4194328
  168.7 0.0 copy-start.1
  168.7 0.9 copy-done.1
  169.6 3.3 %shard_map.122 = (f32[2048,128]{1,0:T(8,128)}, f32[2048,128]{1,0:T(8,128)}) custom-call(bf16[2,512,2048]{2,1,0:T(8,128)(2,1)S(1)} %copy-done, bf16[512,128]{1,0:T(8,128)(2,1)S(1)} %copy-done.1), custom_call_target="tpu_custom_call" | custom-call | tf_op jit(solution)/shard_map/pallas_call | solution.py:803
Async XLA Ops:
  166.6 2.2 %copy-start = (bf16[2,512,2048]{2,1,0:T(8,128)(2,1)S(1)}, bf16[2,512,2048]{2,1,0:T(8,128)(2,1)}, u32[]{:S(2)}) copy-start(bf16[2,512,2048]{2,1,0:T(8,128)(2,1)} %get-tuple-element.9.ef_ref) | copy-start | bytes 12582916
  168.7 0.9 copy-start.1

commit v4 on v3

--- a/solution.py
+++ b/solution.py
@@ -95,8 +95,8 @@
     loss_ref, hg_ref, ef_hbm,
     ebuf, fbuf, head, fce, fcf, pk, rk, ef,
     hpart, hrecv, hmine, hblk, tq, tnorm, dnorm,
-    tl, tl_up, tl_down, dl, dl_up, dl_down, arbuf, lossbuf, inner_out,
-    lgrad, dg, dg_in, dg_up, dg_down, dz, dz_up, dz_down,
+    tl, tl_up, tl_down, dl, dl_up, dl_down, arbuf, lossbuf, staged,
+    lgrad, dg, dg_in, dg_up, dg_down, dz, dz_in,
     zf_up, zf_down, dy, dy_up, dy_down, hg_out, hg,
     send_sems, recv_sems, local_sems,
 ):
@@ -145,19 +145,14 @@
         greet((x, m, around(z, o, Z)))
     for o in range(1, M):
         greet((x, around(m, o, M), z))
-    own_xc = x * C + c
-    for o in range(1, X * C):
-        g = around(own_xc, o, X * C)
-        greet((g // C, y * C + g % C, z))
+    for o in range(1, X):
+        greet((around(x, o, X), m, z))
     off_diagonal = x != y
     for o in range(M):
         if o == 0:
             pl.when(off_diagonal)(lambda: greet((y, m, z)))
         else:
             greet((y, around(m, o, M), z))
-    steady = (Z - 1) + (M - 1) + (X * C - 1) + (X * C - 1)
-    pl.semaphore_wait(barrier, steady + off_diagonal.astype(I32))
-
     start, total = [], jnp.int32(0)
     for k in range(seqs):
         start.append(total)
@@ -176,6 +171,9 @@
     pk[:, :KC] = dot(pick, ebuf[...]).astype(BF)
     loads[1].wait()
     pk[:, KC:] = dot(pick, fbuf[...]).astype(BF)
+
+    steady = (Z - 1) + (M - 1) + (X - 1) + (X * C - 1)
+    pl.semaphore_wait(barrier, steady + off_diagonal.astype(I32))
 
     def slots(k):
         return pl.ds(pl.multiple_of(k * SL, SL), SL)
@@ -201,7 +199,7 @@
     ef[0, my_rows, mine] = dealt[:, :KC]
     ef[1, my_rows, mine] = dealt[:, KC:]
 
-    def plane_gather(name, view, beside=None):
+    def plane_gather(name, view):
         half = Z // 2
         halfy = Y // 2
 
@@ -211,12 +209,23 @@
         def at_y(a):
             return turn(y, a, Y)
 
+        def z_to(o, hop):
+            v = view(y, c, at_z(o))
+            ln.send(v, v, (x, m, at_z(hop)), (name, "z", o - hop))
+
         def z_pass(k):
-            v = view(y, c, at_z(-(k - 1)))
-            ln.send(v, v, (x, m, at_z(1)), (name, "z+", k))
-            if k < half:
-                v = view(y, c, at_z(k - 1))
-                ln.send(v, v, (x, m, at_z(-1)), (name, "z-", k))
+            if Z != 8:
+                z_to(1 - k, 1)
+                if k < half:
+                    z_to(k - 1, -1)
+            elif k == 1:
+                for hop in (1, -1, 2, -2):
+                    z_to(0, hop)
+            elif k == 2:
+                z_to(-1, 2)
+                z_to(1, -2)
+            elif k == 3:
+                z_to(-2, 2)
 
         def across(a, o):
             v = view(at_y(a), c, at_z(o))
@@ -251,7 +260,7 @@
         for k in range(1, half + 3):
             if k <= half:
                 for o in waves[k]:
-                    ln.recv(view(y, c, at_z(o)), (name, "z+" if o < 0 else "z-", abs(o)))
+                    ln.recv(view(y, c, at_z(o)), (name, "z", o))
                 if k < half:
                     z_pass(k + 1)
                 for o in waves[k]:
@@ -262,57 +271,10 @@
             if 0 <= k - 2 <= half:
                 for o in waves[k - 2]:
                     from_y2(o)
-            if beside:
-                beside(k)
         for wave in waves:
             for o in wave:
                 for a in range(Y):
                     ln.recv(view(at_y(a), 1 - c, at_z(o)), (name, "core", a % Y, o % Z))
-
-    def plane_gather_y(name, piece, block):
-        half = Z // 2
-        halfy = Y // 2
-
-        def y_device(a):
-            return (x, turn(y, a, Y) * C + c, z)
-
-        v = piece(y)
-        ln.send(v, v, y_device(1), (name, "y+"))
-        if halfy > 1:
-            ln.send(v, v, y_device(-1), (name, "y-"))
-        yield
-        v = piece(turn(y, -1, Y))
-        ln.recv(v, (name, "y+"))
-        if halfy > 1:
-            ln.send(v, v, y_device(1), (name, "y2"))
-            ln.recv(piece(turn(y, 1, Y)), (name, "y-"))
-            yield
-            ln.recv(piece(turn(y, 2, Y)), (name, "y2"))
-
-        def z_pass(k):
-            v = block(c, turn(z, -(k - 1), Z))
-            ln.send(v, v, (x, m, turn(z, 1, Z)), (name, "z+", k))
-            if k < half:
-                v = block(c, turn(z, k - 1, Z))
-                ln.send(v, v, (x, m, turn(z, -1, Z)), (name, "z-", k))
-
-        def across(o):
-            v = block(c, turn(z, o, Z))
-            ln.send(v, v, sibling, (name, "core", -o % Z))
-
-        z_pass(1)
-        across(0)
-        for k in range(1, half + 1):
-            yield
-            ln.recv(block(c, turn(z, -k, Z)), (name, "z+", k))
-            if k < half:
-                ln.recv(block(c, turn(z, k, Z)), (name, "z-", k))
-                z_pass(k + 1)
-                across(k)
-            across(-k)
-        yield
-        for o in range(Z):
-            ln.recv(block(1 - c, turn(z, o, Z)), (name, "core", o))
 
     class Ring:
         def __init__(self, name, me, n, device, chunk, up, down):
@@ -376,8 +338,50 @@
 
         return second
 
-    def xc_device(g):
-        return (g // C, y * C + g % C, z)
+    class RowSums:
+        def __init__(self, name, base, staged):
+            self.name, self.base, self.staged = name, base, staged
+
+        def first(self, tile):
+            v = arbuf.at[self.base + z]
+            v[...] = tile
+            for o in range(1, Z):
+                ln.send(v, v, (x, m, around(z, o, Z)), (self.name, o))
+
+        def second(self):
+            for o in range(1, Z):
+                ln.recv(arbuf.at[self.base + around(z, -o, Z)], (self.name, o))
+            part = arbuf[self.base]
+            for k in range(1, Z):
+                part = part + arbuf[self.base + k]
+            self.staged[...] = part
+            self.sem = len(ln.tags)
+            for k in range(M):
+                ln.tag((self.name, "from", k))
+            own_slot = arbuf.at[self.base + Z + m]
+            for o in range(X):
+                for other in range(C):
+                    ln.send(
+                        self.staged, own_slot,
+                        (around(x, o, X), x * C + (c + other) % C, z), (self.name, "to", o * C + other),
+                        when=off_diagonal if o == 0 and other == 0 else None, recv_sem=recv_sems.at[self.sem + m],
+                    )
+
+            @pl.when(x == y)
+            def _():
+                own_slot[...] = part
+
+        def third(self):
+            for o in range(M):
+                k = around(m, o, M)
+                ln.recv(
+                    arbuf.at[self.base + Z + k], (self.name, "to", o),
+                    when=off_diagonal if o == 0 else None, recv_sem=recv_sems.at[self.sem + k],
+                )
+            part = arbuf[self.base + Z]
+            for k in range(1, M):
+                part = part + arbuf[self.base + Z + k]
+            return to_columns(part)[:, :1]
 
     def rows_view(yy, cc, zz):
         rows = pl.ds(pl.multiple_of(zz * GROUP, GROUP), GROUP)
@@ -417,6 +421,8 @@
     for k in range(1, X):
         hsum = hsum + hrecv[k]
     hmine[...] = hsum.reshape(Q, LANES)
+    draft_sums = RowSums("dsq", 0, staged.at[0])
+    draft_sums.first(to_rows([jnp.sum(hmine[...] * hmine[...], axis=1, keepdims=True)]))
     ln.send(hmine, hblk, (y, x * C + c, z), "swap", when=off_diagonal)
 
     @pl.when(x == y)
@@ -459,11 +465,11 @@
         target_rings[h].down(1)
 
     target_part(0)
+    draft_sums.second()
+    target_part(1)
     ln.recv(hblk, "swap", when=off_diagonal)
     hid = hblk[...]
-    second = add_up("dsq", to_rows([jnp.sum(hid * hid, axis=1, keepdims=True)]), 0, X * C, own_xc, xc_device)
-    target_part(1)
-    draft_square = to_columns(second()())[:, :1]
+    draft_square = draft_sums.third()
     dscale = lax.rsqrt(draft_square / depth + eps_norm)
     dgain = dgain_ref[pl.ds(c * Z + z, 1), :]
 
@@ -476,17 +482,61 @@
     norm = (hid * dscale * dgain).astype(BF)
     norm_view(0, y, c, z)[...] = norm[:H]
     norm_view(1, y, c, z)[...] = norm[H:]
-    second_gather = plane_gather_y(
-        "norm1", lambda yy: norm_view(1, yy, c, z), lambda cc, zz: dnorm.at[1, :, norm_columns(cc, zz)]
-    )
-    next(second_gather)
-
-    def beside(k):
-        next(second_gather, None)
-        if k in (2, 4):
-            target_rings[k // 2 - 1].up(2)
-
-    plane_gather("norm0", functools.partial(norm_view, 0), beside)
+
+    def norm_block(h, a, cc):
+        columns = pl.ds(pl.multiple_of(cc * side, side), side)
+        return dnorm.at[h, pl.ds(pl.multiple_of(turn(y, a, Y) * H, H), H), columns]
+
+    def y_device(a):
+        return (x, turn(y, a, Y) * C + c, z)
+
+    def norm_across(h, a):
+        v = norm_block(h, a, c)
+        ln.send(v, v, sibling, ("norm core", h, -a % Y))
+
+    def norm_z(h):
+        v = norm_view(h, y, c, z)
+        for o in range(1, Z):
+            ln.send(v, v, (x, m, around(z, o, Z)), ("norm z", h, o))
+
+    def norm_y(h):
+        for o in range(1, Z):
+            ln.recv(norm_view(h, y, c, around(z, -o, Z)), ("norm z", h, o))
+        v = norm_block(h, 0, c)
+        ln.send(v, v, y_device(1), ("norm y", h, 1))
+        if Y > 2:
+            ln.send(v, v, y_device(-1), ("norm y", h, -1))
+        norm_across(h, 0)
+
+    def norm_pass(h):
+        v = norm_block(h, -1, c)
+        ln.recv(v, ("norm y", h, 1))
+        if Y > 2:
+            ln.send(v, v, y_device(1), ("norm y", h, 2))
+        norm_across(h, -1)
+        if Y > 2:
+            ln.recv(norm_block(h, 1, c), ("norm y", h, -1))
+            norm_across(h, 1)
+
+    def norm_last(h):
+        if Y > 2:
+            ln.recv(norm_block(h, 2, c), ("norm y", h, 2))
+            norm_across(h, 2)
+
+    def norm_arrived(h):
+        for a in range(Y):
+            ln.recv(norm_block(h, a, 1 - c), ("norm core", h, a))
+
+    norm_z(0)
+    norm_z(1)
+    norm_y(0)
+    norm_y(1)
+    norm_pass(0)
+    target_rings[0].up(2)
+    norm_pass(1)
+    target_rings[1].up(2)
+    norm_last(0)
+    norm_arrived(0)
 
     def draft_part(h):
         part = dot_last(dnorm[h], head[...])
@@ -495,8 +545,8 @@
     draft_part(0)
     draft_rings[0].up(1)
     draft_rings[0].down(1)
-    for _ in second_gather:
-        pass
+    norm_last(1)
+    norm_arrived(1)
     draft_part(1)
     draft_rings[1].up(1)
 
@@ -535,7 +585,7 @@
             jnp.sum(jnp.where(column == labels[h], draft_logit, 0.0), axis=1, keepdims=True),
         ]
         tile = to_rows([jnp.concatenate([column_sum] * (LANES // H), axis=0) for column_sum in sums])
-        base = Z + X * C + h * (Z + M)
+        base = (1 + h) * (Z + M)
         return add_up(("sums", h), tile, base, M, m, lambda g: (x, g, z))
 
     def logit_grad(h, sums):
@@ -555,50 +605,7 @@
             ln.send(v, v, x_device(turn(x, -1, X)), ("lg", h, -1))
         return jnp.sum(grad.astype(F32) * dl[h, x], axis=1, keepdims=True)
 
-    inner_base = Z + X * C + 2 * (Z + M)
-
-    def inner_first(columns):
-        arbuf[inner_base + z] = to_rows([jnp.concatenate(columns, axis=0)])
-        for o in range(1, Z):
-            v = arbuf.at[inner_base + z]
-            ln.send(v, v, (x, m, around(z, o, Z)), ("inner", o))
-
-    def inner_second():
-        for o in range(1, Z):
-            ln.recv(arbuf.at[inner_base + around(z, -o, Z)], ("inner", o))
-        part = arbuf[inner_base]
-        for k in range(1, Z):
-            part = part + arbuf[inner_base + k]
-        inner_out[...] = part
-        first_name = len(ln.tags)
-        for k in range(M):
-            ln.tag(("inner row", k))
-        for o in range(X):
-            for side_core in range(C):
-                own = o == 0 and side_core == 0
-                ln.send(
-                    inner_out, arbuf.at[inner_base + Z + m],
-                    (around(x, o, X), x * C + (c + side_core) % C, z), ("inner to", o, side_core),
-                    when=off_diagonal if own else None, recv_sem=recv_sems.at[first_name + m],
-                )
-
-        @pl.when(x == y)
-        def _():
-            arbuf[inner_base + Z + m] = inner_out[...]
-
-        return first_name
-
-    def inner_third(first_name):
-        for o in range(M):
-            k = around(m, o, M)
-            ln.recv(
-                arbuf.at[inner_base + Z + k], ("inner to", o // C, o % C),
-                when=off_diagonal if o == 0 else None, recv_sem=recv_sems.at[first_name + k],
-            )
-        part = arbuf[inner_base + Z]
-        for k in range(1, M):
-            part = part + arbuf[inner_base + Z + k]
-        return to_columns(part)[:, :1]
+    inner_sums = RowSums("inner", 3 * (Z + M), staged.at[1])
 
     def row_loss(sums):
         lse = jnp.log(sums[2:3])
@@ -644,10 +651,6 @@
     ring_y1 = Ring(
         "y1", y, Y, lambda i: (x, i * C + c, z), lambda i: dg.at[1, c, i], lambda k: dg_up.at[k], lambda k: dg_down.at[k]
     )
-    ring_z1 = Ring(
-        "z1", z, Z, lambda i: (x, m, i), lambda i: dz.at[i], lambda k: dz_up.at[k], lambda k: dz_down.at[k]
-    )
-
     def step(ring, k):
         ring.up(k)
         ring.down(k)
@@ -659,39 +662,44 @@
     inner_0 = logit_grad(0, sums_0)
     finish_1 = second_1()
     grad_pass(0)
+    grad_arrived(0)
+    other_half(0)
     sums_1 = finish_1()
     inner_1 = logit_grad(1, sums_1)
-    grad_arrived(0)
-    other_half(0)
-    inner_first([inner_0, inner_1])
+    inner_sums.first(to_rows([jnp.concatenate([inner_0, inner_1], axis=0)]))
     own_half(0)
     step(ring_z0, 1)
     grad_pass(1)
     grad_arrived(1)
     other_half(1)
-    inner_name = inner_second()
+    inner_sums.second()
     own_half(1)
     step(ring_y1, 1)
     step(ring_z0, 2)
     lossbuf[x] = jnp.broadcast_to(row_loss(sums_0) + row_loss(sums_1), (8, LANES))
     for o in range(1, X):
         ln.send(lossbuf.at[x], lossbuf.at[x], (around(x, o, X), m, z), ("loss", o))
-    inner = inner_third(inner_name)
+    inner = inner_sums.third()
     ring_y1.up(2)
     step(ring_z0, 3)
     step(ring_z0, 4)
     summed = ring_y1.finish()
     for k in range(Z):
         dz[k] = summed[:, k * LANES:(k + 1) * LANES]
-    step(ring_z1, 1)
+    for o in range(1, Z):
+        to = around(z, o, Z)
+        ln.send(dz.at[to], dz_in.at[z], (x, m, to), ("z1", o))
+    dz_in[z] = dz[z]
     dy[...] = ring_z0.finish()
     step(ring_y0, 1)
-    step(ring_z1, 2)
     ring_y0.up(2)
-    step(ring_z1, 3)
-    step(ring_z1, 4)
     dgrad_0 = ring_y0.finish()
-    dgrad = jnp.concatenate([dgrad_0, ring_z1.finish()], axis=0)
+    for o in range(1, Z):
+        ln.recv(dz_in.at[around(z, -o, Z)], ("z1", o))
+    dgrad_1 = dz_in[0]
+    for k in range(1, Z):
+        dgrad_1 = dgrad_1 + dz_in[k]
+    dgrad = jnp.concatenate([dgrad_0, dgrad_1], axis=0)
 
     upstream = dgrad * dgain
     hid = hblk[...]
@@ -768,11 +776,11 @@
         V((X, R // LANES, 8, LANES), F32), V((R, width), BF), V((2, R // 2, width), BF),
         V((2, X, H, vocab), F32), V((2, half, H, vocab), F32), V((2, rest, H, vocab), F32),
         V((2, X, H, vocab), F32), V((2, half, H, vocab), F32), V((2, rest, H, vocab), F32),
-        V((4 * Z + X * C + 3 * M, 8, LANES), F32), V((X, 8, LANES), F32), V((8, LANES), F32),
+        V((4 * (Z + M), 8, LANES), F32), V((X, 8, LANES), F32), V((2, 8, LANES), F32),
         V((2, X, H, vocab), BF),
         V((2, C, Y, H, side), F32), V((2, Y, H, side), F32),
         V((halfy, H, side), F32), V((resty, H, side), F32),
-        V((Z, H, LANES), F32), V((halfz, H, LANES), F32), V((restz, H, LANES), F32),
+        V((Z, H, LANES), F32), V((Z, H, LANES), F32),
         V((halfz, Y, H, LANES), F32), V((restz, Y, H, LANES), F32),
         V((Y, H, LANES), F32), V((halfy, H, LANES), F32), V((resty, H, LANES), F32),
         V((2, H, LANES), BF), V((2, Y, H, LANES), BF),
@@ -799,7 +807,7 @@
         lengths, offsets, token_ids, target_gain.reshape(1, width), draft_gain.reshape(width // LANES, LANES),
         target_hidden, embeds, head, fc_embed, fc_feature,
     )
-    tile = min(512, width)
+    tile = min(1024, width)
     grad_embed, grad_feature = pl.pallas_call(
         outer,
         grid=(width // tile,),
@@ -809,7 +817,7 @@
             pl.BlockSpec((R, LANES), lambda i: (0, 0)),
         ],
         out_specs=(pl.BlockSpec((tile, LANES), lambda i: (i, 0)), pl.BlockSpec((tile, LANES), lambda i: (i, 0))),
-        compiler_params=pltpu.CompilerParams(vmem_limit_bytes=32 * 1024 * 1024),
+        compiler_params=pltpu.CompilerParams(vmem_limit_bytes=60 * 1024 * 1024),
     )(rows, block_grad)
     return loss[0, 0], grad_embed, grad_feature
 

time: 178 us -> 167 us (0.938)
  Pallas kernels: 169 us -> 162 us
  local copies, waits for them, and re-layouts: 3.08 us -> 0 us
    pallas_call x1, Pallas kernels: 166 us -> 158 us  [on_device(): pl.pallas_call(functools.partial(kernel, (X, M, Z, R)), out_shape=(jax.Sh...]
    unnamed x4 -> x0, local copies, waits for them, and re-layouts: 3.08 us -> none
where the time goes in v4:
time: 167 us; the launch traced here: 164 us
  Pallas kernels  162 us (97%)
  between operations  2.33 us (1%)
    pallas_call x1, Pallas kernels, on_device(): pl.pallas_call(functools.partial(kernel, (X, M, Z, R)), out_shape=(jax.Sh...  158 us
    pallas_call x1, Pallas kernels, on_device(): pl.pallas_call(outer, grid=(width // tile,), out_shape=(jax.ShapeDtypeStr...  4.17 us

profile of v4, /device:TPU:1, one launch (start us, length us, event | category | flops | bytes accessed | tf_op | source)
XLA Modules:
  0.0 164.4 jit_solution(13860370158726277588)
XLA Ops:
  0.6 157.9 %shard_map.121 = (f32[1,1]{1,0:T(1,128)}, bf16[512,128]{1,0:T(8,128)(2,1)}, bf16[2,512,2048]{2,1,0:T(8,128)(2,1)}) custom-call(s32[8]{0:T(128)} %lengths_ref.1, s32[8]{0:T(128)} %offsets_ref.1, s32[8,256]{1,0:T(8,128)} %tokens_ref.1, f32[1,2048]{1,0:T(1,128)} %bitcast.3, f32[16,128]{1,0:T(8,128)} %bitcast.4, bf16[1,256,2048]{2,1,0:T(8,128)(2,1)} %feat_hbm.1, ...), custom_call_target="tpu_custom_call" | custom-call | flops 7500000256 | bytes 10000000 | tf_op jit(solution)/shard_map/pallas_call | solution.py:792
  158.5 4.2 %shard_map.122 = (f32[2048,128]{1,0:T(8,128)}, f32[2048,128]{1,0:T(8,128)}) custom-call(bf16[2,512,2048]{2,1,0:T(8,128)(2,1)} %get-tuple-element.9.ef_ref, bf16[512,128]{1,0:T(8,128)(2,1)} %get-tuple-element.10.hg_ref), custom_call_target="tpu_custom_call" | custom-call | tf_op jit(solution)/shard_map/pallas_call | solution.py:811

commit v5 on v4

--- a/solution.py
+++ b/solution.py
@@ -46,7 +46,7 @@
 class Links:
     def __init__(self, send_sems, recv_sems, peer):
         self.send_sems, self.recv_sems, self.peer = send_sems, recv_sems, peer
-        self.tags, self.started = {}, []
+        self.tags, self.started, self.settled = {}, [], 0
 
     def tag(self, name):
         return self.recv_sems.at[self.tags.setdefault(name, len(self.tags))]
@@ -80,12 +80,13 @@
         else:
             pl.when(when)(copy.wait_recv)
 
-    def finish(self):
-        for copy, when in self.started:
+    def settle(self, count):
+        for copy, when in self.started[self.settled:count]:
             if when is None:
                 copy.wait_send()
             else:
                 pl.when(when)(copy.wait_send)
+        self.settled = count
 
 
 def kernel(
@@ -97,7 +98,7 @@
     hpart, hrecv, hmine, hblk, tq, tnorm, dnorm,
     tl, tl_up, tl_down, dl, dl_up, dl_down, arbuf, lossbuf, staged,
     lgrad, dg, dg_in, dg_up, dg_down, dz, dz_in,
-    zf_up, zf_down, dy, dy_up, dy_down, hg_out, hg,
+    zf_up, zf_down, dy, dy_in, hg_out, hg,
     send_sems, recv_sems, local_sems,
 ):
     X, M, Z, R = sizes
@@ -600,9 +601,8 @@
         grad = grad.astype(BF)
         lgrad[h, x] = grad
         v = lgrad.at[h, x]
-        ln.send(v, v, x_device(turn(x, 1, X)), ("lg", h, 1))
-        if X > 2:
-            ln.send(v, v, x_device(turn(x, -1, X)), ("lg", h, -1))
+        for o in range(1, X):
+            ln.send(v, v, x_device(around(x, o, X)), ("lg", h, o))
         return jnp.sum(grad.astype(F32) * dl[h, x], axis=1, keepdims=True)
 
     inner_sums = RowSums("inner", 3 * (Z + M), staged.at[1])
@@ -616,16 +616,9 @@
             + z_weight * lse * lse
         )
 
-    def grad_pass(h):
-        v = lgrad.at[h, turn(x, -1, X)]
-        ln.recv(v, ("lg", h, 1))
-        if X > 2:
-            ln.send(v, v, x_device(turn(x, 1, X)), ("lg", h, 2))
-
     def grad_arrived(h):
-        if X > 2:
-            ln.recv(lgrad.at[h, turn(x, 1, X)], ("lg", h, -1))
-            ln.recv(lgrad.at[h, turn(x, 2, X)], ("lg", h, 2))
+        for o in range(1, X):
+            ln.recv(lgrad.at[h, around(x, -o, X)], ("lg", h, o))
 
     def grad_part(h, half):
         part = dot(lgrad[h].reshape(HALF, vocab), head[:, pl.ds(pl.multiple_of(half * side, side), side)])
@@ -633,20 +626,19 @@
 
     def other_half(h):
         grad_part(h, 1 - c)
-        ln.send(dg.at[h, 1 - c], dg_in.at[h], sibling, ("dgc", h))
-
-    def own_half(h):
-        grad_part(h, c)
-        ln.recv(dg_in.at[h], ("dgc", h))
-        dg[h, c] += dg_in[h]
+        for o in ((2, 1, -1, 0) if Y > 2 else (1, 0)):
+            i = turn(y, o, Y)
+            ln.send(dg.at[h, 1 - c, i], dg_in.at[h, i], sibling, ("dgc", h, -o % Y))
+
+    def add_other(h, o):
+        i = turn(y, o, Y)
+        ln.recv(dg_in.at[h, i], ("dgc", h, o % Y))
+        dg[h, c, i] += dg_in[h, i]
 
     ring_z0 = Ring(
         "z0", z, Z, lambda i: (x, m, i),
         lambda i: dg.at[0, c, :, :, pl.ds(pl.multiple_of(i * LANES, LANES), LANES)],
         lambda k: zf_up.at[k], lambda k: zf_down.at[k],
-    )
-    ring_y0 = Ring(
-        "y0", y, Y, lambda i: (x, i * C + c, z), lambda i: dy.at[i], lambda k: dy_up.at[k], lambda k: dy_down.at[k]
     )
     ring_y1 = Ring(
         "y1", y, Y, lambda i: (x, i * C + c, z), lambda i: dg.at[1, c, i], lambda k: dg_up.at[k], lambda k: dg_down.at[k]
@@ -661,20 +653,27 @@
     sums_0 = finish_0()
     inner_0 = logit_grad(0, sums_0)
     finish_1 = second_1()
-    grad_pass(0)
     grad_arrived(0)
     other_half(0)
     sums_1 = finish_1()
     inner_1 = logit_grad(1, sums_1)
     inner_sums.first(to_rows([jnp.concatenate([inner_0, inner_1], axis=0)]))
-    own_half(0)
+    grad_part(0, c)
+    for o in range(Y):
+        add_other(0, o)
     step(ring_z0, 1)
-    grad_pass(1)
     grad_arrived(1)
     other_half(1)
+    grad_part(1, c)
+    add_other(1, Y // 2)
+    ring_y1.up(1)
+    if Y > 2:
+        add_other(1, -1)
+        ring_y1.down(1)
+        add_other(1, 1)
+    add_other(1, 0)
     inner_sums.second()
-    own_half(1)
-    step(ring_y1, 1)
+    long_ago = len(ln.started)
     step(ring_z0, 2)
     lossbuf[x] = jnp.broadcast_to(row_loss(sums_0) + row_loss(sums_1), (8, LANES))
     for o in range(1, X):
@@ -682,6 +681,7 @@
     inner = inner_sums.third()
     ring_y1.up(2)
     step(ring_z0, 3)
+    ln.settle(long_ago)
     step(ring_z0, 4)
     summed = ring_y1.finish()
     for k in range(Z):
@@ -691,9 +691,15 @@
         ln.send(dz.at[to], dz_in.at[z], (x, m, to), ("z1", o))
     dz_in[z] = dz[z]
     dy[...] = ring_z0.finish()
-    step(ring_y0, 1)
-    ring_y0.up(2)
-    dgrad_0 = ring_y0.finish()
+    for o in range(1, Y):
+        to = around(y, o, Y)
+        ln.send(dy.at[to], dy_in.at[y], (x, to * C + c, z), ("y0", o))
+    dy_in[y] = dy[y]
+    for o in range(1, Y):
+        ln.recv(dy_in.at[around(y, -o, Y)], ("y0", o))
+    dgrad_0 = dy_in[0]
+    for k in range(1, Y):
+        dgrad_0 = dgrad_0 + dy_in[k]
     for o in range(1, Z):
         ln.recv(dz_in.at[around(z, -o, Z)], ("z1", o))
     dgrad_1 = dz_in[0]
@@ -730,7 +736,7 @@
         ln.recv(hg.at[:, q], None, when=off_diagonal if o == 0 else None, recv_sem=recv_sems.at[first_name + q])
     hg_ref[...] = hg[...].reshape(R, LANES)
     rows_out.wait()
-    ln.finish()
+    ln.settle(len(ln.started))
 
 
 def outer(ef_ref, hg_ref, ge_ref, gf_ref):
@@ -782,7 +788,7 @@
         V((halfy, H, side), F32), V((resty, H, side), F32),
         V((Z, H, LANES), F32), V((Z, H, LANES), F32),
         V((halfz, Y, H, LANES), F32), V((restz, Y, H, LANES), F32),
-        V((Y, H, LANES), F32), V((halfy, H, LANES), F32), V((resty, H, LANES), F32),
+        V((Y, H, LANES), F32), V((Y, H, LANES), F32),
         V((2, H, LANES), BF), V((2, Y, H, LANES), BF),
         pltpu.SemaphoreType.DMA((288,)), pltpu.SemaphoreType.DMA((288,)), pltpu.SemaphoreType.DMA((6,)),
     ]

time: 167 us -> 165 us (0.988)
  Pallas kernels: 162 us -> 160 us
    pallas_call x1, Pallas kernels: 158 us -> 156 us  [on_device(): pl.pallas_call(functools.partial(kernel, (X, M, Z, R)), out_shape=(jax.Sh...]
where the time goes in v5:
time: 165 us; the launch traced here: 162 us
  Pallas kernels  160 us (97%)
  between operations  2.33 us (1%)
    pallas_call x1, Pallas kernels, on_device(): pl.pallas_call(functools.partial(kernel, (X, M, Z, R)), out_shape=(jax.Sh...  156 us
    pallas_call x1, Pallas kernels, on_device(): pl.pallas_call(outer, grid=(width // tile,), out_shape=(jax.ShapeDtypeStr...  4.16 us

profile of v5, /device:TPU:1, one launch (start us, length us, event | category | flops | bytes accessed | tf_op | source)
XLA Modules:
  0.0 162.4 jit_solution(15857357799934120992)
XLA Ops:
  0.6 155.9 %shard_map.121 = (f32[1,1]{1,0:T(1,128)}, bf16[512,128]{1,0:T(8,128)(2,1)}, bf16[2,512,2048]{2,1,0:T(8,128)(2,1)}) custom-call(s32[8]{0:T(128)} %lengths_ref.1, s32[8]{0:T(128)} %offsets_ref.1, s32[8,256]{1,0:T(8,128)} %tokens_ref.1, f32[1,2048]{1,0:T(1,128)} %bitcast.3, f32[16,128]{1,0:T(8,128)} %bitcast.4, bf16[1,256,2048]{2,1,0:T(8,128)(2,1)} %feat_hbm.1, ...), custom_call_target="tpu_custom_call" | custom-call | flops 7500000256 | bytes 10000000 | tf_op jit(solution)/shard_map/pallas_call | solution.py:798
  156.6 4.2 %shard_map.122 = (f32[2048,128]{1,0:T(8,128)}, f32[2048,128]{1,0:T(8,128)}) custom-call(bf16[2,512,2048]{2,1,0:T(8,128)(2,1)} %get-tuple-element.9.ef_ref, bf16[512,128]{1,0:T(8,128)(2,1)} %get-tuple-element.10.hg_ref), custom_call_target="tpu_custom_call" | custom-call | tf_op jit(solution)/shard_map/pallas_call | solution.py:817
